TPU v7x, 32 devices: a whole 2x2x4 slice. The times are simulated.
32 devices in a mesh: dp: 2 (over y), row: 4 (over z), col: 4 (over x, core).
Axes of the slice: x: 2, y: 2, z: 4, core: 2. Of those that a mesh axis runs over, the one named last changes fastest.
Arguments:
- layer_in: bfloat16 [8280, 4, 384], P(('dp', 'col'), 'row'), may hold values from -6 to 6
- grad_out: bfloat16 [8280, 4, 384], P(('dp', 'col'), 'row'), may hold values from -6 to 6
- crop_ids: int32 [16560], P(('dp', 'row')), may hold values from 0 to 239, as said below
- w_qkv: float32 [768, 3, 768], P(('row', 'dp'), None, 'col'), may hold values from -0.21875 to 0.21875
- w_out: float32 [768, 768], P(('col', 'dp'), 'row'), may hold values from -1 to 1
- w_fc1: float32 [768, 3072], P(('row', 'dp'), 'col'), may hold values from -0.21875 to 0.21875
- w_fc2: float32 [3072, 768], P(('col', 'dp'), 'row'), may hold values from -0.109375 to 0.109375
- norm_gains: float32 [1536], replicated, may hold values from 0.4 to 2
- all_biases: float32 [7680], replicated, may hold values from -1.5 to 1.5
- first_qkv: float32 [768, 3, 768], P(('row', 'dp'), None, 'col'), may hold values from -0.0022538076 to 0.0022538076
- second_qkv: float32 [768, 3, 768], P(('row', 'dp'), None, 'col'), may hold values from 7.0550676e-08 to 1.1288108e-06
- first_out: float32 [768, 768], P(('col', 'dp'), 'row'), may hold values from -0.0022538076 to 0.0022538076
- second_out: float32 [768, 768], P(('col', 'dp'), 'row'), may hold values from 7.0550676e-08 to 1.1288108e-06
- first_fc1: float32 [768, 3072], P(('row', 'dp'), 'col'), may hold values from -0.0022538076 to 0.0022538076
- second_fc1: float32 [768, 3072], P(('row', 'dp'), 'col'), may hold values from 7.0550676e-08 to 1.1288108e-06
- first_fc2: float32 [3072, 768], P(('col', 'dp'), 'row'), may hold values from -0.0022538076 to 0.0022538076
- second_fc2: float32 [3072, 768], P(('col', 'dp'), 'row'), may hold values from 7.0550676e-08 to 1.1288108e-06
- first_gains: float32 [1536], replicated, may hold values from -0.0022538076 to 0.0022538076
- second_gains: float32 [1536], replicated, may hold values from 7.0550676e-08 to 1.1288108e-06
- first_biases: float32 [7680], replicated, may hold values from -0.0022538076 to 0.0022538076
- second_biases: float32 [7680], replicated, may hold values from 7.0550676e-08 to 1.1288108e-06
Outputs:
- layer_out: float32 [8280, 4, 384], P(('dp', 'col'), 'row')
- grad_in: float32 [8280, 4, 384], P(('dp', 'col'), 'row')
- grad_norm: float32 [], replicated
- new_first_qkv: float32 [768, 3, 768], P(('row', 'dp'), None, 'col')
- new_second_qkv: float32 [768, 3, 768], P(('row', 'dp'), None, 'col')
- new_w_qkv: float32 [768, 3, 768], P(('row', 'dp'), None, 'col')
- half_w_qkv: bfloat16 [768, 3, 768], P(('row', 'dp'), None, 'col')
- new_first_out: float32 [768, 768], P(('col', 'dp'), 'row')
- new_second_out: float32 [768, 768], P(('col', 'dp'), 'row')
- new_w_out: float32 [768, 768], P(('col', 'dp'), 'row')
- half_w_out: bfloat16 [768, 768], P(('col', 'dp'), 'row')
- new_first_fc1: float32 [768, 3072], P(('row', 'dp'), 'col')
- new_second_fc1: float32 [768, 3072], P(('row', 'dp'), 'col')
- new_w_fc1: float32 [768, 3072], P(('row', 'dp'), 'col')
- half_w_fc1: bfloat16 [768, 3072], P(('row', 'dp'), 'col')
- new_first_fc2: float32 [3072, 768], P(('col', 'dp'), 'row')
- new_second_fc2: float32 [3072, 768], P(('col', 'dp'), 'row')
- new_w_fc2: float32 [3072, 768], P(('col', 'dp'), 'row')
- half_w_fc2: bfloat16 [3072, 768], P(('col', 'dp'), 'row')
- new_first_gains: float32 [1536], replicated
- new_second_gains: float32 [1536], replicated
- new_gains: float32 [1536], replicated
- half_gains: bfloat16 [1536], replicated
- new_first_biases: float32 [7680], replicated
- new_second_biases: float32 [7680], replicated
- new_biases: float32 [7680], replicated
- half_biases: bfloat16 [7680], replicated
Inputs may be any that keep to these rules, and one draw needn't show every extreme that they name: `crop_ids`: tokens come in images of 690 consecutive positions starting at multiples of 690; each image holds 2 crops of 197 tokens and 8 crops of 37 tokens, each crop's tokens consecutive, in an order that varies from image to image; a token's value is its image's index times 10 plus its crop's place within the image.
All inputs are finite; a program needn't handle non-finite values.
Results may differ from a plain program's by a relative error of at most 0.019.
Values may be sent and summed in bfloat16 or wider, within the bound.
A program may use at most 256 MiB of HBM per device.

v0:
```python
import jax
import jax.numpy as jnp
from jax import lax
from jax.sharding import PartitionSpec as P

HEAD_DIM = 64
FF = 3072
D = 768
BIG_CROP = 197
BIG_COUNT = 2
IMAGE_LEN = 690
CROPS = 10
STEP = 5


NORM_EPS = 1e-06
CLIP_NORM = 1.0
BETA_ONE = 0.5
BETA_TWO = 0.5
ADAM_EPS = 1e-08
DECAY = 0.05
MASKED = -1e30


def as_sent(array):
    return jax.tree.map(lambda a: a.astype(jnp.bfloat16) if a.dtype == jnp.float32 else a, array)


def unpack_rows(value):
    return value.reshape(value.shape[0] * 2, value.shape[2] // 2)


def pack_rows(value):
    return value.reshape(value.shape[0] // 2, 1, value.shape[1] * 2)


def cols_in(value):
    return lax.all_gather(value, "col", axis=0, tiled=True)


def rows_in(value):
    return lax.all_gather(as_sent(value), "row", axis=0, tiled=True).astype(value.dtype)


def product(left, weight, flipped):
    if flipped:
        return lax.dot_general(
            left, weight, (((1,), (1,)), ((), ())), preferred_element_type=jnp.float32
        )
    return jnp.dot(left, weight, preferred_element_type=jnp.float32)


def rows_out(whole, weight, flipped):
    return lax.psum_scatter(
        product(
            lax.dynamic_slice_in_dim(
                whole,
                jnp.int32(0),
                lax.axis_size("row") * (whole.shape[0] // lax.axis_size("row")),
                0,
            ),
            weight,
            flipped,
        ),
        "row",
        scatter_dimension=0,
        tiled=True,
    )


def cols_out(whole, weight, flipped):
    return lax.psum_scatter(
        product(
            lax.dynamic_slice_in_dim(
                whole,
                jnp.int32(0),
                whole.shape[0] // lax.axis_size("col") * lax.axis_size("col"),
                0,
            ),
            weight,
            flipped,
        ).astype(jnp.bfloat16),
        "col",
        scatter_dimension=0,
        tiled=True,
    ).astype(jnp.float32)


def contract_rows(left, right):
    return lax.dot_general(
        left, right, (((0,), (0,)), ((), ())), preferred_element_type=jnp.float32
    )


def piece_of(vector, start, count):
    return lax.dynamic_slice_in_dim(vector, start, count, 0)


def place_in(vector, piece, start):
    return lax.dynamic_update_slice_in_dim(vector, piece, start, 0)


def norm_stats(value):
    feature_count = value.shape[1] * lax.axis_size("row")
    row_total = lax.psum(jnp.sum(value, axis=1, keepdims=True), "row")
    centred = value - row_total / feature_count
    spread = lax.psum(jnp.sum(centred * centred, axis=1, keepdims=True), "row") / feature_count
    inverse = lax.rsqrt(spread + NORM_EPS)
    return (centred * inverse, inverse)


def norm_back(grad_norm_out, normed, inverse, gain_part):
    weighted = grad_norm_out * gain_part
    first_sum = jnp.sum(weighted, axis=1, keepdims=True)
    second_sum = jnp.sum(weighted * normed, axis=1, keepdims=True)
    feature_count = normed.shape[1]
    feature_count = normed.shape[1] * lax.axis_size("row")
    first_sum, second_sum = lax.psum((first_sum, second_sum), "row")
    return inverse * (weighted - first_sum / feature_count - normed * (second_sum / feature_count))


def crop_order(labels):
    crop_place = labels % CROPS
    one_hot = (crop_place[:, None] == jnp.arange(CROPS, dtype=jnp.int32)[None, :]).astype(jnp.int32)
    crop_sizes = jnp.sum(one_hot, axis=0)
    tok_length = jnp.sum(one_hot * crop_sizes[None, :], axis=1)
    sort_key = jnp.where(tok_length == BIG_CROP, 0, CROPS) + crop_place
    ordering = jnp.argsort(sort_key, stable=True)
    restore = jnp.argsort(ordering)
    return (ordering, restore)


def block_bounds():
    split_row = BIG_COUNT * BIG_CROP
    return ((0, split_row), (split_row, IMAGE_LEN))


def crop_scores(queries, keys, labels):
    scores = jnp.einsum(
        "qhd,khd->hqk", queries, keys, preferred_element_type=jnp.float32
    ) * queries.shape[2] ** (-0.5)
    same_crop = (labels[:, None] == labels[None, :])[None]
    return jnp.where(same_crop, scores, MASKED)


def attend_block(queries, keys, values, labels):
    scores = crop_scores(queries, keys, labels)
    peak = jnp.max(scores, axis=2, keepdims=True)
    expd = jnp.exp(scores - peak)
    totals = jnp.sum(expd, axis=2, keepdims=True)
    weights = (expd / totals).astype(jnp.bfloat16)
    mixed = jnp.einsum("hqk,khd->qhd", weights, values, preferred_element_type=jnp.float32)
    return (mixed, peak + jnp.log(totals))


def attend(pieces):
    queries, keys, values, labels = pieces
    ordering, restore = crop_order(labels)
    sorted_q = jnp.take(queries, ordering, axis=0)
    sorted_k = jnp.take(keys, ordering, axis=0)
    sorted_v = jnp.take(values, ordering, axis=0)
    sorted_l = jnp.take(labels, ordering, axis=0)
    mixed_parts = []
    total_parts = []
    for start_row, stop_row in block_bounds():
        mixed, log_totals = attend_block(
            sorted_q[start_row:stop_row],
            sorted_k[start_row:stop_row],
            sorted_v[start_row:stop_row],
            sorted_l[start_row:stop_row],
        )
        mixed_parts.append(mixed)
        total_parts.append(log_totals)
    mixed = jnp.take(jnp.concatenate(mixed_parts, axis=0), restore, axis=0)
    return (mixed.astype(jnp.bfloat16), jnp.concatenate(total_parts, axis=1))


def attend_back_block(queries, keys, values, labels, log_totals, grad_mixed):
    factor_scale = queries.shape[2] ** (-0.5)
    weights = jnp.exp(crop_scores(queries, keys, labels) - log_totals)
    grad_weights = jnp.einsum(
        "qhd,khd->hqk", grad_mixed, values, preferred_element_type=jnp.float32
    )
    grad_scores = (
        weights * (grad_weights - jnp.sum(weights * grad_weights, axis=2, keepdims=True))
    ).astype(jnp.bfloat16)
    grad_query = (
        jnp.einsum("hqk,khd->qhd", grad_scores, keys, preferred_element_type=jnp.float32)
        * factor_scale
    )
    grad_key = (
        jnp.einsum("hqk,qhd->khd", grad_scores, queries, preferred_element_type=jnp.float32)
        * factor_scale
    )
    grad_value = jnp.einsum(
        "hqk,qhd->khd", weights.astype(jnp.bfloat16), grad_mixed, preferred_element_type=jnp.float32
    )
    return (grad_query, grad_key, grad_value)


def attend_back(pieces):
    queries, keys, values, labels, log_totals, grad_mixed = pieces
    ordering, restore = crop_order(labels)
    sorted_q = jnp.take(queries, ordering, axis=0)
    sorted_k = jnp.take(keys, ordering, axis=0)
    sorted_v = jnp.take(values, ordering, axis=0)
    sorted_l = jnp.take(labels, ordering, axis=0)
    sorted_g = jnp.take(grad_mixed, ordering, axis=0)
    query_parts = []
    key_parts = []
    value_parts = []
    for start_row, stop_row in block_bounds():
        grad_query, grad_key, grad_value = attend_back_block(
            sorted_q[start_row:stop_row],
            sorted_k[start_row:stop_row],
            sorted_v[start_row:stop_row],
            sorted_l[start_row:stop_row],
            log_totals[:, start_row:stop_row],
            sorted_g[start_row:stop_row],
        )
        query_parts.append(grad_query)
        key_parts.append(grad_key)
        value_parts.append(grad_value)
    grad_query = jnp.take(jnp.concatenate(query_parts, axis=0), restore, axis=0)
    grad_key = jnp.take(jnp.concatenate(key_parts, axis=0), restore, axis=0)
    grad_value = jnp.take(jnp.concatenate(value_parts, axis=0), restore, axis=0)
    return (grad_query, grad_key, grad_value)


def run_attention(qkv_half, labels_flat, tok_local, width):
    images = tok_local // IMAGE_LEN
    heads_here = width // HEAD_DIM
    queries = qkv_half[:, 0].reshape(images, IMAGE_LEN, heads_here, HEAD_DIM)
    keys = qkv_half[:, 1].reshape(images, IMAGE_LEN, heads_here, HEAD_DIM)
    values = qkv_half[:, 2].reshape(images, IMAGE_LEN, heads_here, HEAD_DIM)
    labels = labels_flat.reshape(images, IMAGE_LEN)
    mixed, log_totals = lax.map(attend, (queries, keys, values, labels))
    return ((queries, keys, values, labels, log_totals), mixed.reshape(tok_local, width))


def run_attention_back(kept, grad_mixed, tok_local, width):
    queries, keys, values, labels, log_totals = kept
    images = tok_local // IMAGE_LEN
    heads_here = width // HEAD_DIM
    grad_query, grad_key, grad_value = lax.map(
        attend_back,
        (
            queries,
            keys,
            values,
            labels,
            log_totals,
            grad_mixed.reshape(images, IMAGE_LEN, heads_here, HEAD_DIM),
        ),
    )
    return jnp.stack(
        [
            grad_query.reshape(tok_local, width),
            grad_key.reshape(tok_local, width),
            grad_value.reshape(tok_local, width),
        ],
        axis=1,
    ).astype(jnp.bfloat16)


def adam_step(weight, grad, first, second, rate, factor):
    clipped = grad * factor
    new_first = BETA_ONE * first + (1.0 - BETA_ONE) * clipped
    new_second = BETA_TWO * second + (1.0 - BETA_TWO) * clipped * clipped
    unbiased_first = new_first / (1.0 - BETA_ONE**STEP)
    unbiased_second = new_second / (1.0 - BETA_TWO**STEP)
    new_weight = weight - rate * (
        unbiased_first / (jnp.sqrt(unbiased_second) + ADAM_EPS) + DECAY * weight
    )
    return (new_first, new_second, new_weight, new_weight.astype(jnp.bfloat16))


def gelu_exact(pre_act):
    return jax.nn.gelu(pre_act, approximate=False)


def local(
    layer_in,
    grad_out,
    crop_ids,
    w_qkv,
    w_out,
    w_fc1,
    w_fc2,
    norm_gains,
    all_biases,
    first_qkv,
    second_qkv,
    first_out,
    second_out,
    first_fc1,
    second_fc1,
    first_fc2,
    second_fc2,
    first_gains,
    second_gains,
    first_biases,
    second_biases,
):
    row_index = lax.axis_index("row")
    col_index = lax.axis_index("col")
    tok_local = crop_ids.shape[0]
    feat_rows = layer_in.shape[2] // 2
    tokens_flat = unpack_rows(layer_in)
    cotangent = unpack_rows(grad_out)
    head_cols = w_qkv.shape[2]
    hidden_cols = w_fc1.shape[1]
    row_start = row_index * feat_rows
    head_start = col_index * head_cols
    hidden_start = col_index * hidden_cols
    gain_one = piece_of(norm_gains, row_start, feat_rows)
    gain_two = piece_of(norm_gains, D + row_start, feat_rows)
    shift_one = piece_of(all_biases, row_start, feat_rows)
    shift_two = piece_of(all_biases, D + row_start, feat_rows)
    bias_query = piece_of(all_biases, 2 * D + head_start, head_cols)
    bias_value = piece_of(all_biases, 3 * D + head_start, head_cols)
    bias_out = piece_of(all_biases, 4 * D + row_start, feat_rows)
    bias_fc2 = piece_of(all_biases, 5 * D + row_start, feat_rows)
    bias_fc1 = piece_of(all_biases, 6 * D + hidden_start, hidden_cols)
    wide_qkv, wide_out, wide_fc1, wide_fc2 = (
        lax.all_gather(w_qkv.astype(jnp.bfloat16), "dp", axis=0, tiled=True),
        lax.all_gather(w_out.astype(jnp.bfloat16), "dp", axis=0, tiled=True),
        lax.all_gather(w_fc1.astype(jnp.bfloat16), "dp", axis=0, tiled=True),
        lax.all_gather(w_fc2.astype(jnp.bfloat16), "dp", axis=0, tiled=True),
    )
    flat_qkv = wide_qkv.reshape(feat_rows, 3 * head_cols)
    inputs = tokens_flat.astype(jnp.float32)
    normed_one, inverse_one = norm_stats(inputs)
    act_one = (normed_one * gain_one + shift_one).astype(jnp.bfloat16)
    one_rows = cols_in(act_one)
    qkv_sum = rows_out(one_rows, flat_qkv, False).reshape(tok_local, 3, head_cols)
    qkv_sum = qkv_sum + jnp.stack([bias_query, jnp.zeros_like(bias_query), bias_value])
    qkv_half = qkv_sum.astype(jnp.bfloat16)
    kept, mixed_half = run_attention(qkv_half, crop_ids, tok_local, head_cols)
    mixed_rows = rows_in(mixed_half)
    middle = inputs + cols_out(mixed_rows, wide_out, False) + bias_out
    normed_two, inverse_two = norm_stats(middle)
    act_two = (normed_two * gain_two + shift_two).astype(jnp.bfloat16)
    two_rows = cols_in(act_two)
    hidden = rows_out(two_rows, wide_fc1, False) + bias_fc1
    active, gelu_pull = jax.vjp(gelu_exact, hidden)
    active_half = active.astype(jnp.bfloat16)
    active_rows = rows_in(active_half)
    out_rows_final = middle + cols_out(active_rows, wide_fc2, False) + bias_fc2
    active_rows = rows_in(lax.optimization_barrier(active_half))
    two_rows = cols_in(lax.optimization_barrier(act_two))
    mixed_rows = rows_in(lax.optimization_barrier(mixed_half))
    one_rows = cols_in(lax.optimization_barrier(act_one))
    out_rows = cols_in(cotangent)
    grad_fc2 = contract_rows(active_rows, out_rows)
    grad_active = rows_out(out_rows, wide_fc2, True)
    grad_hidden = gelu_pull(grad_active)[0].astype(jnp.bfloat16)
    hidden_rows = rows_in(grad_hidden)
    grad_fc1 = contract_rows(two_rows, hidden_rows)
    grad_two = cols_out(hidden_rows, wide_fc1, True)
    grad_middle = cotangent.astype(jnp.float32) + norm_back(
        grad_two, normed_two, inverse_two, gain_two
    )
    branch_half = grad_middle.astype(jnp.bfloat16)
    branch_rows = cols_in(branch_half)
    grad_outw = contract_rows(mixed_rows, branch_rows)
    grad_mixed = rows_out(branch_rows, wide_out, True).astype(jnp.bfloat16)
    grad_qkv = run_attention_back(kept, grad_mixed, tok_local, head_cols)
    qkv_rows = rows_in(grad_qkv.reshape(tok_local, 3 * head_cols))
    grad_qkvw = contract_rows(one_rows, qkv_rows).reshape(feat_rows, 3, head_cols)
    grad_one = cols_out(qkv_rows, flat_qkv, True)
    grad_rows_final = grad_middle + norm_back(grad_one, normed_one, inverse_one, gain_one)
    gains_part = jnp.zeros((2 * D,), jnp.float32)
    gains_part = place_in(gains_part, jnp.sum(grad_one * normed_one, axis=0), row_start)
    gains_part = place_in(gains_part, jnp.sum(grad_two * normed_two, axis=0), D + row_start)
    biases_part = jnp.zeros((6 * D + FF,), jnp.float32)
    biases_part = place_in(biases_part, jnp.sum(grad_one, axis=0), row_start)
    biases_part = place_in(biases_part, jnp.sum(grad_two, axis=0), D + row_start)
    biases_part = place_in(
        biases_part, jnp.sum(grad_qkv[:, 0].astype(jnp.float32), axis=0), 2 * D + head_start
    )
    biases_part = place_in(
        biases_part, jnp.sum(grad_qkv[:, 2].astype(jnp.float32), axis=0), 3 * D + head_start
    )
    biases_part = place_in(
        biases_part, jnp.sum(branch_half.astype(jnp.float32), axis=0), 4 * D + row_start
    )
    biases_part = place_in(
        biases_part, jnp.sum(cotangent.astype(jnp.float32), axis=0), 5 * D + row_start
    )
    biases_part = place_in(
        biases_part, jnp.sum(grad_hidden.astype(jnp.float32), axis=0), 6 * D + hidden_start
    )
    owned_qkv, owned_out, owned_fc1, owned_fc2 = (
        lax.psum_scatter(
            grad_qkvw.astype(jnp.bfloat16), "dp", scatter_dimension=0, tiled=True
        ).astype(jnp.float32),
        lax.psum_scatter(
            grad_outw.astype(jnp.bfloat16), "dp", scatter_dimension=0, tiled=True
        ).astype(jnp.float32),
        lax.psum_scatter(
            grad_fc1.astype(jnp.bfloat16), "dp", scatter_dimension=0, tiled=True
        ).astype(jnp.float32),
        lax.psum_scatter(
            grad_fc2.astype(jnp.bfloat16), "dp", scatter_dimension=0, tiled=True
        ).astype(jnp.float32),
    )
    local_squares = (
        jnp.sum(owned_qkv * owned_qkv)
        + jnp.sum(owned_out * owned_out)
        + jnp.sum(owned_fc1 * owned_fc1)
        + jnp.sum(owned_fc2 * owned_fc2)
    )
    grad_gains, grad_biases, weight_squares = lax.psum(
        (gains_part, biases_part, local_squares), ("dp", "row", "col")
    )
    grad_norm = jnp.sqrt(
        weight_squares + jnp.sum(grad_gains * grad_gains) + jnp.sum(grad_biases * grad_biases)
    )
    factor = jnp.minimum(1.0, CLIP_NORM / grad_norm)
    upd_qkv = adam_step(w_qkv, owned_qkv, first_qkv, second_qkv, D ** (-0.5), factor)
    upd_out = adam_step(w_out, owned_out, first_out, second_out, (D // 24) ** (-0.5), factor)
    upd_fc1 = adam_step(w_fc1, owned_fc1, first_fc1, second_fc1, D ** (-0.5), factor)
    upd_fc2 = adam_step(w_fc2, owned_fc2, first_fc2, second_fc2, FF ** (-0.5), factor)
    upd_gains = adam_step(norm_gains, grad_gains, first_gains, second_gains, 0.3, factor)
    upd_biases = adam_step(all_biases, grad_biases, first_biases, second_biases, 0.3, factor)
    return (
        pack_rows(out_rows_final),
        pack_rows(grad_rows_final),
        grad_norm,
        upd_qkv[0],
        upd_qkv[1],
        upd_qkv[2],
        upd_qkv[3],
        upd_out[0],
        upd_out[1],
        upd_out[2],
        upd_out[3],
        upd_fc1[0],
        upd_fc1[1],
        upd_fc1[2],
        upd_fc1[3],
        upd_fc2[0],
        upd_fc2[1],
        upd_fc2[2],
        upd_fc2[3],
        upd_gains[0],
        upd_gains[1],
        upd_gains[2],
        upd_gains[3],
        upd_biases[0],
        upd_biases[1],
        upd_biases[2],
        upd_biases[3],
    )


def solution(mesh):
    return jax.shard_map(
        local,
        mesh=mesh,
        in_specs=(
            P(("dp", "col"), "row", None),
            P(("dp", "col"), "row", None),
            P(("dp", "row")),
            P(("row", "dp"), None, "col"),
            P(("col", "dp"), "row"),
            P(("row", "dp"), "col"),
            P(("col", "dp"), "row"),
            P(),
            P(),
            P(("row", "dp"), None, "col"),
            P(("row", "dp"), None, "col"),
            P(("col", "dp"), "row"),
            P(("col", "dp"), "row"),
            P(("row", "dp"), "col"),
            P(("row", "dp"), "col"),
            P(("col", "dp"), "row"),
            P(("col", "dp"), "row"),
            P(),
            P(),
            P(),
            P(),
        ),
        out_specs=(
            P(("dp", "col"), "row", None),
            P(("dp", "col"), "row", None),
            P(),
            P(("row", "dp"), None, "col"),
            P(("row", "dp"), None, "col"),
            P(("row", "dp"), None, "col"),
            P(("row", "dp"), None, "col"),
            P(("col", "dp"), "row"),
            P(("col", "dp"), "row"),
            P(("col", "dp"), "row"),
            P(("col", "dp"), "row"),
            P(("row", "dp"), "col"),
            P(("row", "dp"), "col"),
            P(("row", "dp"), "col"),
            P(("row", "dp"), "col"),
            P(("col", "dp"), "row"),
            P(("col", "dp"), "row"),
            P(("col", "dp"), "row"),
            P(("col", "dp"), "row"),
            P(),
            P(),
            P(),
            P(),
            P(),
            P(),
            P(),
            P(),
        ),
        check_vma=False,
    )
```

profile of v0, /device:TPU:0, one launch (start us, length us, event | category | flops | bytes accessed | tf_op | source)
XLA Modules:
  0.0 3567.8 jit_solution(8484114889226853492)
XLA Ops:
  9.3 13.9 psum.77
  24.0 8.7 psum.78
  37.8 5.8 all_gather.49
  43.8 23.4 all-gather.25.cloned.1.call-done
  67.2 6.2 copy.200
  73.4 6.5 reshape.428
  79.9 9.9 fusion.101
  92.5 636.3 %all-reduce.20.cloned.1.call-done = f32[8280,576]{0,1:T(8,128)} async-done(((f32[8280,576]{0,1:T(8,128)}), f32[8280,576]{0,1:T(8,128)}) %all-reduce.20.cloned.1.call-update) | async-done | bytes 19077136
  753.6 134.5 %while.30 = (s32[]{:T(128)}, bf16[3,690,3,64]{3,2,1,0:T(4,128)(2,1)}, f32[3,3,690,1]{2,1,3,0:T(4,128)}, bf16[3,690,3,64]{3,2,1,0:T(4,128)(2,1)}, s32[3,690]{1,0:...) while((s32[]{:T(128)}, bf16[3,690,3,64]{3,2,1,0:T(4,128)(2,1)}, ...), condition=%wide.region_14.18_spmd, body=%wide.region_5.17_spmd.sunk | while | flops 195584304 | bytes 21094596 | solution.py:237
  899.6 4.8 all_gather.51
  904.4 5.8 all_gather.55
  910.2 49.7 %all-gather.27.cloned.1.call-done = bf16[4,2070,192]{1,2,0:T(8,128)(2,1)} async-done(((bf16[1,2070,192]{1,2,0:T(8,128)(2,1)}), bf16[4,2070,192]{1,2,0:T(8,128)(2,1)}) %all-gather.27.cloned.1.call-update) | async-done | bytes 3179536 | tf_op jit(solution)/shard_map/all_gather | solution.py:42
  959.9 6.3 copy.206
  966.2 6.7 reshape.430
  972.9 4.7 convolution_convert_fusion.2
  977.7 6.1 all_gather.53
  985.0 5.1 all-gather.33.cloned.1.call-done
  990.1 6.3 copy.212
  996.4 6.7 reshape.436
  1003.1 14.2 fusion.103
  1017.3 44.6 %all-reduce.22.cloned.1.call-done = bf16[8280,192]{0,1:T(8,128)(2,1)} async-done(((bf16[8280,192]{0,1:T(8,128)(2,1)}), bf16[8280,192]{0,1:T(8,128)(2,1)}) %all-reduce.22.cloned.1.call-update) | async-done | bytes 3179536
  1067.9 12.1 psum.79
  1082.3 8.7 psum.80
  1095.3 420.1 %fusion.1 = f32[2072,768]{1,0:T(8,128)} fusion(f32[8280,768]{1,0:T(8,128)} %fusion.103), kind=kCustom, calls=%all-reduce-scatter.1 | all-reduce-scatter fusion | flops 6365185 | bytes 31801856
  1518.4 6.2 copy.209
  1524.6 6.9 reshape.432
  1531.4 13.8 fusion.102
  1545.3 417.5 %fusion = f32[2072,768]{1,0:T(8,128)} fusion(f32[8280,768]{1,0:T(8,128)} %fusion.102), kind=kCustom, calls=%all-reduce-scatter | all-reduce-scatter fusion | flops 6365185 | bytes 31801856
  1967.5 16.9 concatenate.31
  1984.4 16.9 concatenate.30
  2001.3 19.8 convert_reduce_fusion.2
  2021.4 221.4 %all-gather.35.cloned.1.call-done = bf16[4,2070,768]{2,1,0:T(8,128)(2,1)} async-done(((bf16[1,2070,768]{2,1,0:T(8,128)(2,1)}), bf16[4,2070,768]{2,1,0:T(8,128)(2,1)}) %all-gather.35.cloned.1.call-update) | async-done | bytes 12718096 | tf_op jit(solution)/shard_map/all_gather | solution.py:42
  2242.8 12.6 reshape.438
  2255.3 10.6 convolution_convert_fusion
  2268.9 64.8 %all-reduce.24.cloned.1.call-done = bf16[8280,192]{0,1:T(8,128)(2,1)} async-done(((bf16[8280,192]{0,1:T(8,128)(2,1)}), bf16[8280,192]{0,1:T(8,128)(2,1)}) %all-reduce.24.cloned.1.call-update) | async-done | bytes 3179536
  2341.6 18.9 all-reduce.12
  2371.5 4.6 reshape.487
  2380.9 7.6 multiply_convert_fusion.2
  2389.2 5.9 all-gather.37.cloned.1.call-done
  2395.1 6.2 copy.215
  2401.3 5.4 reshape.440
  2410.4 362.0 %all-reduce.27 = bf16[8280,192]{0,1:T(8,128)(2,1)} all-reduce(f32[8280,192]{0,1:T(8,128)} %fusion.104), channel_id=8, replica_groups=mesh['dp'=2,'row'=4,'col'=4] {'row'}, use_global_device_ids=true, to_apply=%region_28.32.clone | all-reduce | flops 1589760 | bytes 9538560
  2776.2 201.3 %while.31 = (s32[]{:T(128)}, bf16[3,690,3,64]{3,2,1,0:T(4,128)(2,1)}, bf16[3,690,3,64]{3,2,1,0:T(4,128)(2,1)}, bf16[3,690,3,64]{3,2,1,0:T(4,128)(2,1)}, bf16[3,6...) while((s32[]{:T(128)}, ...), condition=%wide.region_36.40_spmd, body=%wide.region_29.39_spmd.sunk | while | flops 476200640 | bytes 81138048 | solution.py:245
  2785.0 4.4 sort.93
  2851.8 4.4 sort.93
  2919.0 4.4 sort.93
  2996.7 4.6 copy.226
  3005.4 4.6 copy.229
  3014.2 4.5 copy.231
  3023.0 12.6 reshape.450
  3035.7 7.3 convolution_convert_fusion.5
  3044.0 9.0 convolution_convert_fusion.4
  3053.3 52.9 %all-gather.31.cloned.1.call-done = bf16[4,2070,768]{2,1,0:T(8,128)(2,1)} async-done(((bf16[1,2070,768]{2,1,0:T(8,128)(2,1)}), bf16[4,2070,768]{2,1,0:T(8,128)(2,1)}) %all-gather.31.cloned.1.call-update) | async-done | bytes 12718096 | tf_op jit(solution)/shard_map/all_gather | solution.py:42
  3106.2 13.5 reshape.434
  3119.7 10.8 convolution_convert_fusion.1
  3132.3 149.9 %all-gather.39.cloned.1.call-done = bf16[4,2070,576]{1,2,0:T(8,128)(2,1)} async-done(((bf16[1,2070,576]{1,2,0:T(8,128)(2,1)}), bf16[4,2070,576]{1,2,0:T(8,128)(2,1)}) %all-gather.39.cloned.1.call-update) | async-done | bytes 9538576 | tf_op jit(solution)/shard_map/all_gather | solution.py:42
  3282.3 14.2 copy.223
  3296.5 17.3 reshape.442
  3313.7 7.9 convolution_convert_fusion.6
  3322.2 8.2 convolution_convert_fusion.3
  3345.4 116.6 %all-reduce.26.cloned.1.call-done = (bf16[8280,192]{0,1:T(8,128)(2,1)}, bf16[8280,192]{0,1:T(8,128)(2,1)}) async-done(((bf16[8280,192]{0,1:T(8,128)(2,1)}, bf16[8280,192]{0,1:T(8,128)(2,1)}), (bf16[8280,192]{0,1:T(8,128)(2,1)}, bf16[8280,192]{0,1:T(8,128)(2,1)})) %all-reduce.26.cloned.1.call-update) | async-done | bytes 6359056
  3478.6 19.2 all-reduce.11
  3498.0 4.4 fusion.63
  3509.0 38.5 %all-reduce.10 = (f32[]{:T(128)}, f32[1536]{0:T(1024)S(1)}, f32[7680]{0:T(1024)S(1)}) all-reduce(f32[]{:T(128)S(6)} %add.434, f32[1536]{0:T(1024)S(1)} %dynamic_update_slice.61, f32[7680]{0:T(1024)S(1)} %dynamic_update_slice.68), channel_id=1, replica_groups=mesh['dp'=2,'row'=4,'col'=4] {'dp','row','col'}, use_global_device_ids=true, to_apply=%region_50.54 | all-reduce | flops 9217 | bytes 73736 | tf_op jit(solution)/shard_map/psum | solution.py:414
  (702 shorter events, 502.4 us)
Async XLA Ops:
  7.2 60.0 %all-gather.25.cloned.1.call-start = ((), (), s32[]{:S(2)}) async-start(), calls=%async_computation.6 | async-start | bytes 4177920 | tf_op jit(solution)/shard_map/all_gather | solution.py:38
  8.9 2359.2 %copy-start.6 = (f32[2070,192]{1,0:T(8,128)}, f32[2070,192]{1,0:T(8,128)S(1)}, u32[]{:S(2)}) copy-start(f32[2070,192]{1,0:T(8,128)S(1)} %reshape.309) | copy-start | bytes 4769284
  23.3 12.7 copy-start.42
  37.7 691.1 %all-reduce.20.cloned.1.call-start = ((), (), s32[]{:S(2)}) async-start(), calls=%async_computation.20 | async-start | bytes 38338560
  43.8 36.1 %copy-start.22 = (bf16[192,3,192]{0,2,1:T(8,128)(2,1)}, bf16[192,3,192]{0,2,1:T(8,128)(2,1)S(1)}, u32[]{:S(2)}) copy-start(bf16[192,3,192]{0,2,1:T(8,128)(2,1)S(1)} %copy.201) | copy-start | bytes 663556
  89.8 870.1 %all-gather.27.cloned.1.call-start = ((), (), s32[]{:S(2)}) async-start(), calls=%async_computation.7 | async-start | bytes 4177920 | tf_op jit(solution)/shard_map/all_gather | solution.py:42
  790.0 7.1 copy-start.37
  834.8 7.1 copy-start.37
  879.7 7.1 copy-start.37
  894.1 96.1 %all-gather.33.cloned.1.call-start = ((), (), s32[]{:S(2)}) async-start(), calls=%async_computation.10 | async-start | bytes 4177920 | tf_op jit(solution)/shard_map/all_gather | solution.py:38
  897.6 164.2 %all-reduce.22.cloned.1.call-start = ((), (), s32[]{:S(2)}) async-start(), calls=%async_computation.21 | async-start | bytes 6389760
  904.4 68.5 %copy-start.34 = (bf16[192,192]{1,0:T(8,128)(2,1)}, bf16[192,192]{1,0:T(8,128)(2,1)S(1)}, u32[]{:S(2)}) copy-start(bf16[192,192]{1,0:T(8,128)(2,1)S(1)} %all_gather.51) | copy-start | bytes 221188
  910.2 92.9 %copy-start.24 = (bf16[768,192]{0,1:T(8,128)(2,1)}, bf16[768,192]{0,1:T(8,128)(2,1)S(1)}, u32[]{:S(2)}) copy-start(bf16[768,192]{0,1:T(8,128)(2,1)S(1)} %all_gather.55) | copy-start | bytes 884740
  977.6 6.2 copy-start.81
  977.6 540.7 %all-gather.29.cloned.1.call-start = ((), (), s32[]{:S(2)}) async-start(), calls=%async_computation.8 | async-start | bytes 4177920 | tf_op jit(solution)/shard_map/all_gather | solution.py:38
  1017.3 48.9 %copy-start.71 = (f32[192]{0:T(256)S(1)}, f32[192]{0:T(256)}, u32[]{:S(2)}) copy-start(f32[192]{0:T(256)} %get-tuple-element.518) | copy-start | bytes 2308
  1066.2 24.9 copy-start.64
  1066.2 24.9 copy-start.67
  1095.2 1147.6 %all-gather.35.cloned.1.call-start = ((), (), s32[]{:S(2)}) async-start(), calls=%async_computation.11 | async-start | bytes 15912960 | tf_op jit(solution)/shard_map/all_gather | solution.py:42
  1516.1 451.4 %collective-permute-start.1 = (f32[6,768]{1,0:T(8,128)S(1)}, f32[6,768]{1,0:T(8,128)S(1)}, u32[]{:S(2)}, u32[]{:S(2)}) collective-permute-start(f32[6,768]{1,0:T(8,128)S(1)} %slice.188), channel_id=1, source_target_pairs={{0,4},{4,8},{8,12},{1,5},{5,9},{9,13},{2,6},{6,10},{10,14},{3,7},{... | collective-permute-start | bytes 55304
  1963.6 20.8 collective-permute-start
  2021.2 312.6 %all-reduce.24.cloned.1.call-start = ((), (), s32[]{:S(2)}) async-start(), calls=%async_computation.22 | async-start | bytes 6389760
  2266.0 129.1 %all-gather.37.cloned.1.call-start = ((), (), s32[]{:S(2)}) async-start(), calls=%async_computation.12 | async-start | bytes 4177920 | tf_op jit(solution)/shard_map/all_gather | solution.py:38
  2368.0 628.7 %all-gather.41.cloned.1.call-start = ((), (), s32[]{:S(2)}) async-start(), calls=%async_computation.14 | async-start | bytes 4177920 | tf_op jit(solution)/shard_map/all_gather | solution.py:38
  2371.1 6.9 copy-start.8
  2371.1 634.3 %all-gather.43.cloned.1.call-start = ((), (), s32[]{:S(2)}) async-start(), calls=%async_computation.15 | async-start | bytes 4177920 | tf_op jit(solution)/shard_map/all_gather | solution.py:42
  2377.9 636.3 %all-gather.45.cloned.1.call-start = ((), (), s32[]{:S(2)}) async-start(), calls=%async_computation.16 | async-start | bytes 4177920 | tf_op jit(solution)/shard_map/all_gather | solution.py:38
  2380.9 642.1 %all-gather.47.cloned.1.call-start = ((), (), s32[]{:S(2)}) async-start(), calls=%async_computation.17 | async-start | bytes 15912960 | tf_op jit(solution)/shard_map/all_gather | solution.py:42
  2388.5 717.7 %all-gather.31.cloned.1.call-start = ((), (), s32[]{:S(2)}) async-start(), calls=%async_computation.9 | async-start | bytes 15912960 | tf_op jit(solution)/shard_map/all_gather | solution.py:42
  2389.1 893.1 %all-gather.39.cloned.1.call-start = ((), (), s32[]{:S(2)}) async-start(), calls=%async_computation.13 | async-start | bytes 12533760 | tf_op jit(solution)/shard_map/all_gather | solution.py:42
  2806.0 6.5 copy-start.16
  2872.8 6.5 copy-start.16
  2940.0 6.5 copy-start.16
  2996.7 337.2 %reduce-scatter.25.cloned.1.call-start = ((), (), s32[]{:S(2)}) async-start(), calls=%async_computation.19 | async-start | bytes 589824
  3023.0 12.7 copy-start.18
  3044.0 291.7 %reduce-scatter.21.cloned.1.call-start = ((), (), s32[]{:S(2)}) async-start(), calls=%async_computation.5 | async-start | bytes 442368 | tf_op jit(solution)/shard_map/reduce_scatter | solution.py:401
  3053.0 66.7 %copy-start.25 = (bf16[768,192]{0,1:T(8,128)(2,1)S(1)}, bf16[768,192]{0,1:T(8,128)(2,1)}, u32[]{:S(2)}) copy-start(bf16[768,192]{0,1:T(8,128)(2,1)} %copy-done.24) | copy-start | bytes 884740
  3053.0 286.6 %reduce-scatter.19.cloned.1.call-start = ((), (), s32[]{:S(2)}) async-start(), calls=%async_computation.4 | async-start | bytes 147456 | tf_op jit(solution)/shard_map/reduce_scatter | solution.py:398
  3119.7 10.8 copy-start.15
  3119.7 10.8 copy-start.19
  3132.3 208.8 %reduce-scatter.23.cloned.1.call-start = ((), (), s32[]{:S(2)}) async-start(), calls=%async_computation.18 | async-start | bytes 368640
  3296.4 17.3 copy-start.21
  3313.7 8.4 copy-start.23
  3321.7 140.3 %all-reduce.26.cloned.1.call-start = ((), (), s32[]{:S(2)}) async-start(), calls=%async_computation.23 | async-start | bytes 12779520
  3337.2 129.1 %copy-start.9 = (f32[2070,192]{1,0:T(8,128)S(1)}, f32[2070,192]{1,0:T(8,128)}, u32[]{:S(2)}) copy-start(f32[2070,192]{1,0:T(8,128)} %get-tuple-element.487) | copy-start | bytes 4769284
  3337.2 129.1 %copy-start.70 = (f32[192]{0:T(256)S(1)}, f32[192]{0:T(256)}, u32[]{:S(2)}) copy-start(f32[192]{0:T(256)} %get-tuple-element.516) | copy-start | bytes 2308
  3497.9 6.1 copy-start.74
  3498.0 6.4 copy-start.73
  3498.0 6.6 copy-start.65
  3502.4 48.3 %copy-start.29 = (f32[96,3,192]{0,2,1:T(8,128)S(1)}, f32[96,3,192]{0,2,1:T(8,128)}, u32[]{:S(2)}) copy-start(f32[96,3,192]{0,2,1:T(8,128)} %copy.235) | copy-start | bytes 663556
  3502.4 48.3 %copy-start.30 = (f32[96,3,192]{0,2,1:T(8,128)S(1)}, f32[96,3,192]{0,2,1:T(8,128)}, u32[]{:S(2)}) copy-start(f32[96,3,192]{0,2,1:T(8,128)} %copy.233) | copy-start | bytes 663556
  3502.4 48.3 %copy-start.31 = (f32[96,3,192]{0,2,1:T(8,128)S(1)}, f32[96,3,192]{0,2,1:T(8,128)}, u32[]{:S(2)}) copy-start(f32[96,3,192]{0,2,1:T(8,128)} %copy.232) | copy-start | bytes 663556
  3509.0 45.5 %copy-start.27 = (f32[384,192]{0,1:T(8,128)S(1)}, f32[384,192]{0,1:T(8,128)}, u32[]{:S(2)}) copy-start(f32[384,192]{0,1:T(8,128)} %param.37) | copy-start | bytes 884740
  3509.0 45.5 %copy-start.49 = (f32[384,192]{0,1:T(8,128)S(1)}, f32[384,192]{0,1:T(8,128)}, u32[]{:S(2)}) copy-start(f32[384,192]{0,1:T(8,128)} %param.47) | copy-start | bytes 884740
  3509.0 45.5 %copy-start.50 = (f32[384,192]{0,1:T(8,128)S(1)}, f32[384,192]{0,1:T(8,128)}, u32[]{:S(2)}) copy-start(f32[384,192]{0,1:T(8,128)} %param.46) | copy-start | bytes 884740
  3551.0 6.0 copy-start.58
  3551.0 6.7 copy-start.45
  3551.1 6.7 copy-start.55
  3551.1 6.7 copy-start.56
  3551.1 6.7 copy-start.57
  3551.1 7.4 copy-start.28
  3551.1 7.4 copy-start.41
  3551.1 7.4 copy-start.51
  3551.1 7.4 copy-start.52
  (72 other events, 198.2 us)
Sparse Core Ops, SparseCore 0:
  37.8 29.2 all-gather.24
  89.9 638.8 all-reduce.19
  894.2 65.6 all-gather.26
  961.9 28.2 all-gather.32
  992.4 69.4 all-reduce.21
  1095.3 28.3 all-gather.28
  2021.3 221.4 all-gather.34
  2266.1 67.5 all-reduce.23
  2368.1 26.9 all-gather.36
  2396.5 29.6 all-gather.40
  2427.8 120.2 all-gather.42
  2549.5 28.3 all-gather.44
  2579.5 304.8 all-gather.46
  2885.8 220.3 all-gather.30
  3107.6 174.6 all-gather.38
  3284.9 11.2 reduce-scatter.24
  3299.0 12.0 reduce-scatter.20
  3313.8 9.9 reduce-scatter.18
  3326.7 11.4 reduce-scatter.22
  3340.6 121.3 all-reduce.25
where the time goes:
time: 3580 us; the launch traced here: 3570 us
  waiting for transfers between devices  1370 us (38%)
  blocking collectives  1340 us (37%)
  local copies, waits for them, and re-layouts  520 us (15%)
  other arithmetic  172 us (5%)
  matrix products  129 us (4%)
    unnamed x3, blocking collectives  1200 us
    unnamed x28, waiting for transfers between devices  863 us
    all_gather x6, waiting for transfers between devices, rows_in(): lax.all_gather(as_sent(value), 'row', axis=0, tiled=True)  474 us
    unnamed x174, local copies, waits for them, and re-layouts  182 us
  transfers between devices with their start and end apart: 22, of which 11 were waited for; matrix products, arithmetic and copies ran while one was open for 37% of the time, Pallas kernels for 0%

commit v1 on v0

v1 whole, which is shorter than its diff:
```python
import jax
import jax.numpy as jnp
from jax import lax
from jax.sharding import PartitionSpec as P

HEADS = 12
HEAD_DIM = 64
FF = 3072
D = 768
BIG_CROP = 197
SMALL_CROP = 37
IMAGE_LEN = 690
CROPS = 10
STEP = 5

NORM_EPS = 1e-06
CLIP_NORM = 1.0
BETA_ONE = 0.5
BETA_TWO = 0.5
ADAM_EPS = 1e-08
DECAY = 0.05
MASKED = -1e30

SLOTS = 544
BIG_SLOTS = 208
TRIO_SLOTS = 112
TRIO = 3 * SMALL_CROP
BF = jnp.bfloat16
F32 = jnp.float32


def crop_starts(labels):
    images = labels.shape[0] // IMAGE_LEN
    places = labels.reshape(images, IMAGE_LEN) % CROPS
    order = jnp.arange(CROPS, dtype=jnp.int32)
    sizes = jnp.sum((places[:, :, None] == order).astype(jnp.int32), axis=1)
    starts = jnp.sum((places[:, :, None] < order).astype(jnp.int32), axis=1)
    starts = starts + IMAGE_LEN * jnp.arange(images, dtype=jnp.int32)[:, None]
    big = (sizes == BIG_CROP).astype(jnp.int32)
    earlier = (order[:, None] < order[None, :]).astype(jnp.int32)
    big_rank = jnp.sum(big[:, :, None] * earlier, axis=1)
    small_rank = jnp.sum((1 - big)[:, :, None] * earlier, axis=1)

    def ranked(flag, rank, count):
        hit = flag[:, :, None] * (rank[:, :, None] == jnp.arange(count, dtype=jnp.int32)).astype(jnp.int32)
        return jnp.sum(hit * starts[:, :, None], axis=1).reshape(-1)

    return ranked(big, big_rank, 2), ranked(1 - big, small_rank, CROPS - 2)


def slot_segments(kind):
    if kind == 0:
        bigs, trios = 2, 1
    else:
        bigs, trios = 1, 3
    parts = []
    at = 0
    for b in range(bigs):
        parts.append((at, BIG_CROP, True, b))
        at += BIG_SLOTS
    for s in range(3 * trios):
        parts.append((at + s // 3 * TRIO_SLOTS + s % 3 * SMALL_CROP, SMALL_CROP, False, s))
    return parts


def slot_sources(labels):
    big, small = crop_starts(labels)
    rows = []
    for row in range(4):
        kind = row // 2
        at_big = (0, 2, 4, 5)[row]
        at_small = (0, 3, 6, 15)[row]
        out = []
        filled = 0
        for first, length, is_big, index in slot_segments(kind):
            if first > filled:
                out.append(jnp.full((first - filled,), -1, jnp.int32))
            start = big[at_big + index] if is_big else small[at_small + index]
            out.append(start + jnp.arange(length, dtype=jnp.int32))
            filled = first + length
        if filled < SLOTS:
            out.append(jnp.full((SLOTS - filled,), -1, jnp.int32))
        rows.append(jnp.concatenate(out))
    return jnp.stack(rows)


def slot_crops(kind):
    slot = jnp.arange(SLOTS, dtype=jnp.int32)
    crop = jnp.full((SLOTS,), -1, jnp.int32)
    for number, (first, length, _, _) in enumerate(slot_segments(kind)):
        crop = jnp.where((slot >= first) & (slot < first + length), number, crop)
    return crop


def dot(a, b):
    return jnp.dot(a, b, preferred_element_type=F32)


def dot_nt(a, b):
    return lax.dot_general(a, b, (((1,), (1,)), ((), ())), preferred_element_type=F32)


def dot_tn(a, b):
    return lax.dot_general(a, b, (((0,), (0,)), ((), ())), preferred_element_type=F32)


def norm_stats(value):
    centre = jnp.mean(value, axis=1, keepdims=True)
    centred = value - centre
    spread = jnp.mean(centred * centred, axis=1, keepdims=True)
    inverse = lax.rsqrt(spread + NORM_EPS)
    return centred * inverse, inverse


def norm_back(grad, normed, inverse, gain):
    weighted = grad * gain
    first = jnp.mean(weighted, axis=1, keepdims=True)
    second = jnp.mean(weighted * normed, axis=1, keepdims=True)
    return inverse * (weighted - first - normed * second)


def layer(x, cot, crops, w_qkv, w_out, w_fc1, w_fc2, gains, biases):
    inputs = x.astype(F32)
    cotf = cot.astype(F32)
    normed_one, inverse_one = norm_stats(inputs)
    act_one = (normed_one * gains[:D] + biases[:D]).astype(BF)
    qkv_bias = jnp.concatenate([biases[2 * D : 3 * D], jnp.zeros((D,), F32), biases[3 * D : 4 * D]])
    qkv = (dot(act_one, w_qkv) + qkv_bias).astype(BF)
    heads = qkv.reshape(SLOTS, 3, HEADS, HEAD_DIM)
    q, k, v = heads[:, 0], heads[:, 1], heads[:, 2]
    scores = jnp.einsum("qhd,khd->hqk", q, k, preferred_element_type=F32) * HEAD_DIM ** (-0.5)
    scores = jnp.where((crops[:, None] == crops[None, :])[None], scores, MASKED)
    probs = jax.nn.softmax(scores, axis=2)
    half_probs = probs.astype(BF)
    mixed = jnp.einsum("hqk,khd->qhd", half_probs, v, preferred_element_type=F32)
    mixed = mixed.reshape(SLOTS, D).astype(BF)
    middle = inputs + dot(mixed, w_out) + biases[4 * D : 5 * D]
    normed_two, inverse_two = norm_stats(middle)
    act_two = (normed_two * gains[D:] + biases[D : 2 * D]).astype(BF)
    hidden = dot(act_two, w_fc1) + biases[6 * D :]
    active, gelu_pull = jax.vjp(lambda h: jax.nn.gelu(h, approximate=False), hidden)
    active = active.astype(BF)
    out = middle + dot(active, w_fc2) + biases[5 * D : 6 * D]

    g_fc2 = dot_tn(active, cot)
    grad_hidden = gelu_pull(dot_nt(cot, w_fc2))[0].astype(BF)
    g_fc1 = dot_tn(act_two, grad_hidden)
    grad_two = dot_nt(grad_hidden, w_fc1)
    grad_middle = cotf + norm_back(grad_two, normed_two, inverse_two, gains[D:])
    branch = grad_middle.astype(BF)
    g_out = dot_tn(mixed, branch)
    grad_mixed = dot_nt(branch, w_out).astype(BF).reshape(SLOTS, HEADS, HEAD_DIM)
    grad_probs = jnp.einsum("qhd,khd->hqk", grad_mixed, v, preferred_element_type=F32)
    grad_scores = (probs * (grad_probs - jnp.sum(probs * grad_probs, axis=2, keepdims=True))).astype(BF)
    scale = HEAD_DIM ** (-0.5)
    grad_q = jnp.einsum("hqk,khd->qhd", grad_scores, k, preferred_element_type=F32) * scale
    grad_k = jnp.einsum("hqk,qhd->khd", grad_scores, q, preferred_element_type=F32) * scale
    grad_v = jnp.einsum("hqk,qhd->khd", half_probs, grad_mixed, preferred_element_type=F32)
    grad_qkv = jnp.stack([grad_q, grad_k, grad_v], axis=1).astype(BF).reshape(SLOTS, 3 * D)
    g_qkv = dot_tn(act_one, grad_qkv)
    grad_one = dot_nt(grad_qkv, w_qkv)
    grad_in = grad_middle + norm_back(grad_one, normed_one, inverse_one, gains[:D])

    g_gains = jnp.concatenate([jnp.sum(grad_one * normed_one, axis=0), jnp.sum(grad_two * normed_two, axis=0)])
    qkv_sums = jnp.sum(grad_qkv.astype(F32), axis=0)
    g_biases = jnp.concatenate([
        jnp.sum(grad_one, axis=0),
        jnp.sum(grad_two, axis=0),
        qkv_sums[:D],
        qkv_sums[2 * D :],
        jnp.sum(branch.astype(F32), axis=0),
        jnp.sum(cotf, axis=0),
        jnp.sum(grad_hidden.astype(F32), axis=0),
    ])
    return out, grad_in, g_qkv, g_out, g_fc1, g_fc2, g_gains, g_biases


def adam_step(weight, grad, first, second, rate, factor):
    clipped = grad * factor
    new_first = BETA_ONE * first + (1.0 - BETA_ONE) * clipped
    new_second = BETA_TWO * second + (1.0 - BETA_TWO) * clipped * clipped
    unbiased_first = new_first / (1.0 - BETA_ONE**STEP)
    unbiased_second = new_second / (1.0 - BETA_TWO**STEP)
    new_weight = weight - rate * (
        unbiased_first / (jnp.sqrt(unbiased_second) + ADAM_EPS) + DECAY * weight
    )
    return (new_first, new_second, new_weight, new_weight.astype(BF))


def gather(value, axes):
    for name, dim in axes:
        value = lax.all_gather(value, name, axis=dim, tiled=True)
    return value


def scatter(value, axes):
    for name, dim in axes:
        value = lax.psum_scatter(value, name, scatter_dimension=dim, tiled=True)
    return value.astype(F32)


def local(
    layer_in, grad_out, crop_ids, w_qkv, w_out, w_fc1, w_fc2, norm_gains, all_biases,
    first_qkv, second_qkv, first_out, second_out, first_fc1, second_fc1, first_fc2, second_fc2,
    first_gains, second_gains, first_biases, second_biases,
):
    row = lax.axis_index("row")
    n_row, n_col = lax.axis_size("row"), lax.axis_size("col")
    feat = D // n_row
    pairs = layer_in.shape[0]
    labels = lax.ppermute(
        crop_ids, ("row", "col"), [(r * n_col + c, c * n_row + r) for r in range(n_row) for c in range(n_col)]
    )
    sources = slot_sources(labels).reshape(-1)
    place = jnp.where(sources < 0, -1, (sources % 2) * pairs + sources // 2)
    pick = (place[:, None] == jnp.arange(2 * pairs, dtype=jnp.int32)[None, :]).astype(BF)

    def to_slots(value):
        halves = jnp.concatenate([value[:, 0, :feat], value[:, 0, feat:]], axis=0)
        sent = dot(pick, halves).astype(BF)
        got = lax.all_to_all(sent, "row", 0, 0, tiled=True)
        return got.reshape(n_row, SLOTS, feat).transpose(1, 0, 2).reshape(SLOTS, D)

    def to_tokens(value):
        sent = value.astype(BF).reshape(SLOTS, n_row, feat).transpose(1, 0, 2).reshape(n_row * SLOTS, feat)
        got = lax.all_to_all(sent, "row", 0, 0, tiled=True)
        halves = dot_tn(pick, got)
        return jnp.concatenate([halves[:pairs], halves[pairs:]], axis=1).reshape(pairs, 1, 2 * feat)

    full_qkv = gather(w_qkv.astype(BF), (("dp", 0), ("row", 0), ("col", 2))).reshape(D, 3 * D)
    full_out = gather(w_out.astype(BF), (("dp", 0), ("col", 0), ("row", 1)))
    full_fc1 = gather(w_fc1.astype(BF), (("dp", 0), ("row", 0), ("col", 1)))
    full_fc2 = gather(w_fc2.astype(BF), (("dp", 0), ("col", 0), ("row", 1)))
    crops = jnp.where(row < 2, slot_crops(0), slot_crops(1))
    out, grad_in, g_qkv, g_out, g_fc1, g_fc2, g_gains, g_biases = layer(
        to_slots(layer_in), to_slots(grad_out), crops, full_qkv, full_out, full_fc1, full_fc2, norm_gains, all_biases
    )
    owned_qkv = scatter(g_qkv.astype(BF).reshape(D, 3, D), (("col", 2), ("row", 0), ("dp", 0)))
    owned_out = scatter(g_out.astype(BF), (("row", 1), ("col", 0), ("dp", 0)))
    owned_fc1 = scatter(g_fc1.astype(BF), (("col", 1), ("row", 0), ("dp", 0)))
    owned_fc2 = scatter(g_fc2.astype(BF), (("row", 1), ("col", 0), ("dp", 0)))
    local_squares = (
        jnp.sum(owned_qkv * owned_qkv)
        + jnp.sum(owned_out * owned_out)
        + jnp.sum(owned_fc1 * owned_fc1)
        + jnp.sum(owned_fc2 * owned_fc2)
    )
    grad_gains, grad_biases, weight_squares = lax.psum((g_gains, g_biases, local_squares), ("dp", "row", "col"))
    grad_norm = jnp.sqrt(weight_squares + jnp.sum(grad_gains * grad_gains) + jnp.sum(grad_biases * grad_biases))
    factor = jnp.minimum(1.0, CLIP_NORM / grad_norm)
    upd_qkv = adam_step(w_qkv, owned_qkv, first_qkv, second_qkv, D ** (-0.5), factor)
    upd_out = adam_step(w_out, owned_out, first_out, second_out, (D // 24) ** (-0.5), factor)
    upd_fc1 = adam_step(w_fc1, owned_fc1, first_fc1, second_fc1, D ** (-0.5), factor)
    upd_fc2 = adam_step(w_fc2, owned_fc2, first_fc2, second_fc2, FF ** (-0.5), factor)
    upd_gains = adam_step(norm_gains, grad_gains, first_gains, second_gains, 0.3, factor)
    upd_biases = adam_step(all_biases, grad_biases, first_biases, second_biases, 0.3, factor)
    return (
        to_tokens(out), to_tokens(grad_in), grad_norm,
        *upd_qkv, *upd_out, *upd_fc1, *upd_fc2, *upd_gains, *upd_biases,
    )


def solution(mesh):
    tokens = P(("dp", "col"), "row", None)
    qkv = P(("row", "dp"), None, "col")
    out = P(("col", "dp"), "row")
    fc1 = P(("row", "dp"), "col")
    whole = P()
    return jax.shard_map(
        local,
        mesh=mesh,
        in_specs=(
            tokens, tokens, P(("dp", "row")), qkv, out, fc1, out, whole, whole,
            qkv, qkv, out, out, fc1, fc1, out, out, whole, whole, whole, whole,
        ),
        out_specs=(tokens, tokens, whole) + (qkv,) * 4 + (out,) * 4 + (fc1,) * 4 + (out,) * 4 + (whole,) * 8,
        check_vma=False,
    )
```

time: 3580 us -> 809 us (0.23)
  blocking collectives: 1340 us -> 114 us
  waiting for transfers between devices: 1370 us -> 341 us
  local copies, waits for them, and re-layouts: 520 us -> 74 us
  other arithmetic: 172 us -> 84.7 us
    unnamed x3 -> x0, blocking collectives: 1200 us -> none
    unnamed x28 -> x23, waiting for transfers between devices: 863 us -> 55.5 us
    all_gather x12 -> x6, waiting for transfers between devices: 508 us -> 33.9 us  [gather(): value = lax.all_gather(value, name, axis=dim, tiled=True)]
    reduce_scatter x2 -> x7, waiting for transfers between devices: 0.01 us -> 193 us  [scatter(): value = lax.psum_scatter(value, name, scatter_dimension=dim, tiled=True)]
    gather x60 -> x0, local copies, waits for them, and re-layouts: 149 us -> none  [the longest x6 15.7 us: attend(): sorted_k = jnp.take(keys, ordering, axis=0)]
    unnamed x174 -> x164, local copies, waits for them, and re-layouts: 182 us -> 36.6 us
    psum x7 -> x1, blocking collectives: 120 us -> 40.1 us  [local(): lax.psum((g_gains, g_biases, local_squares), ('dp', 'row', 'col'))]
    all_to_all x0 -> x4, waiting for transfers between devices: none -> 58.9 us  [the longest x2 50.4 us: to_slots(): got = lax.all_to_all(sent, 'row', 0, 0, tiled=True)]
  transfers between devices with their start and end apart: 22 -> 23, of which waited for: 11 -> 15; matrix products, arithmetic and copies ran while one was open for 37% -> 25% of each run, Pallas kernels for 0% -> 0%
where the time goes in v1:
time: 809 us; the launch traced here: 800 us
  waiting for transfers between devices  341 us (42%)
  matrix products  141 us (17%)
  blocking collectives  114 us (14%)
  other arithmetic  84.7 us (10%)
  local copies, waits for them, and re-layouts  74 us (9%)
  starting transfers between devices  24.3 us (3%)
  between operations  21.6 us (3%)
    reduce_scatter x7, waiting for transfers between devices, scatter(): value = lax.psum_scatter(value, name, scatter_dimension=dim, tiled=True)  193 us
    all_gather x6, blocking collectives, gather(): value = lax.all_gather(value, name, axis=dim, tiled=True)  74 us
    unnamed x23, waiting for transfers between devices  55.5 us
    all_to_all x2, waiting for transfers between devices, to_slots(): got = lax.all_to_all(sent, 'row', 0, 0, tiled=True)  50.4 us
    psum x1, blocking collectives, local(): lax.psum((g_gains, g_biases, local_squares), ('dp', 'row', 'col'))  40.1 us
    unnamed x164, local copies, waits for them, and re-layouts  36.6 us
    dot_general x4, matrix products, dot_nt(): lax.dot_general(a, b, (((1,), (1,)), ((), ())), preferred_element_type=F32)  36.2 us
    all_gather x6, waiting for transfers between devices, gather(): value = lax.all_gather(value, name, axis=dim, tiled=True)  33.9 us
  transfers between devices with their start and end apart: 23, of which 15 were waited for; matrix products, arithmetic and copies ran while one was open for 25% of the time, Pallas kernels for 0%

profile of v1, /device:TPU:0, one launch (start us, length us, event | category | flops | bytes accessed | tf_op | source)
XLA Modules:
  0.0 800.4 jit_solution(2190716641440790143)
XLA Ops:
  8.2 7.6 all_gather.42
  16.9 5.9 all_gather.45
  24.0 6.3 all_gather.36
  30.4 42.9 %all_gather.37 = bf16[768,3,192]{2,1,0:T(4,128)(2,1)S(1)} all-gather(bf16[192,3,192]{2,1,0:T(4,128)(2,1)S(1)} %all_gather.36), channel_id=1, replica_groups=mesh['dp'=2,'row'=4,'col'=4] {'row'}, dimensions={0}, use_global_device_ids=true | all-gather | bytes 1105920 | tf_op jit(solution)/shard_map/all_gather | solution.py:192
  73.3 2.0 copy.225
  75.4 4.8 all_gather.39
  80.2 6.4 all_gather.40
  112.1 4.2 fusion.23
  118.3 9.3 %all-to-all-start = ((bf16[4,544,192]{1,2,0:T(8,128)(2,1)}), bf16[4,544,192]{1,2,0:T(8,128)(2,1)S(1)}, u32[]{:S(2)}, u32[]{:S(2)}) async-start(bf16[4,544,192]{1,2,0:T(8,128)(2,1)} %copy.223), calls=%async_computation | async-start | bytes 1966080 | tf_op jit(solution)/shard_map/all_to_all | solution.py:221
  128.0 4.2 fusion.24
  134.2 32.2 %all-to-all-done = bf16[4,544,192]{1,2,0:T(8,128)(2,1)S(1)} async-done(((bf16[4,544,192]{1,2,0:T(8,128)(2,1)}), bf16[4,544,192]{1,2,0:T(8,128)(2,1)S(1)}, u32[]{:S(2)}, u32[]{:S(2)}) %all-to-all-start) | async-done | bytes 835616 | tf_op jit(solution)/shard_map/all_to_all | solution.py:221
  166.4 3.5 all-to-all-start.2
  173.5 2.8 copy.229
  176.3 18.3 %all-to-all-done.2 = bf16[4,544,192]{1,2,0:T(8,128)(2,1)S(1)} async-done(((bf16[4,544,192]{1,2,0:T(8,128)(2,1)}), bf16[4,544,192]{1,2,0:T(8,128)(2,1)S(1)}, u32[]{:S(2)}, u32[]{:S(2)}) %all-to-all-start.2) | async-done | bytes 835616 | tf_op jit(solution)/shard_map/all_to_all | solution.py:221
  197.2 6.1 add_convert_fusion.1
  203.2 4.0 copy.226
  207.3 7.4 fusion.43
  214.7 20.9 %fusion.117 = (f32[12,544]{1,0:T(8,128)S(1)}, f32[12,544,544]{1,2,0:T(8,128)}) fusion(f32[12,544,544]{1,2,0:T(8,128)} %fusion.43, pred[544,544]{0,1:T(8,128)(4,1)S(1)} %broadcast_compare_fusion), kind=kOutput, calls=%fused_computation.287 | output fusion | flops 21307936 | bytes 28731904 | tf_op jit(solution)/shard_map/sub | solution.py:133
  235.6 8.6 %fusion.25 = bf16[12,64,544]{2,1,0:T(8,128)(2,1)} fusion(bf16[544,3,12,64]{0,3,2,1:T(8,128)(2,1)S(1)} %bitcast.137, f32[12,544,544]{1,2,0:T(8,128)} %get-tuple-element.284, f32[12,544]{1,0:T(8,128)S(1)} %get-tuple-element.283), kind=kOutput, calls=%fused_computation.71 | convolution fusion | flops 462077952 | bytes 16064512 | tf_op jit(solution)/shard_map/hqk,khd->qhd/dot_general | solution.py:135
  244.1 3.2 fusion.118
  248.9 8.5 %fusion.95 = f32[544,3072]{1,0:T(8,128)} fusion(bf16[768,3072]{1,0:T(8,128)(2,1)} %all-gather.13.cloned.1.call-done, f32[544,768]{1,0:T(8,128)} %copy-done.5, f32[768]{0:T(1024)S(1)} %get-tuple-element.244, f32[768]{0:T(1024)S(1)} %get-tuple-element.251, f32[544]{0:T(1024)S(1)} %add_rsqrt_fusion, f32[544]{0:T(1024)S(1)} %broadcast_multiply_fusion.4), kind=kOutput, calls=%fused_computation.272 | convolution fusion | flops 2569003008 | bytes 13084928 | tf_op jit(solution)/shard_map/dot_general | solution.py:96
  257.4 33.8 %all-gather.17.cloned.1.call-done = bf16[3072,768]{0,1:T(8,128)(2,1)} async-done(((bf16[3072,192]{0,1:T(8,128)(2,1)}), bf16[3072,768]{0,1:T(8,128)(2,1)}) %all-gather.17.cloned.1.call-update) | async-done | bytes 4718608 | tf_op jit(solution)/shard_map/all_gather | solution.py:192
  291.2 22.4 %convert_reduce_fusion = (f32[3072]{0:T(1024)}, bf16[544,3072]{1,0:T(8,128)(2,1)S(1)}, f32[544,3072]{1,0:T(8,128)}) fusion(f32[544,3072]{1,0:T(8,128)} %fusion.95, f32[3072]{0:T(1024)S(1)} %slice.218, bf16[544,768]{0,1:T(8,128)(2,1)} %bitcast.143, bf16[3072,768]{0,1:T(8,128)(2,1)} %all-gather.17.cloned.1.call-done), kind=kOutput, calls=%fused_computation.21 | convolution fusion | flops 2692248576 | bytes 22290432 | tf_op jit(solution)/shard_map/dot_general | solution.py:100
  313.6 3.7 multiply_reduce_fusion.2
  319.7 2.2 convolution_convert_fusion.3
  321.9 3.5 convolution_convert_fusion.4
  325.4 2.2 copy.234
  327.6 11.0 %multiply_reduce_fusion = (f32[12,544]{1,0:T(8,128)S(1)}, f32[12,544,544]{1,2,0:T(8,128)}) fusion(f32[12,544,544]{1,2,0:T(8,128)} %get-tuple-element.284, f32[12,544]{1,0:T(8,128)S(1)} %get-tuple-element.283, bf16[544,12,64]{0,2,1:T(8,128)(2,1)} %bitcast.150, bf16[544,3,12,64]{0,3,2,1:T(8,128)(2,1)S(1)} %bitcast.138), kind=kOutput, calls=%fused_computation.7 | convolution fusion | flops 465204864 | bytes 30295552 | tf_op jit(solution)/shard_map/qhd,khd->hqk/dot_general | solution.py:153
  338.6 11.4 %multiply_convert_fusion = bf16[12,544,544]{1,2,0:T(8,128)(2,1)S(1)} fusion(f32[12,544,544]{1,2,0:T(8,128)} %get-tuple-element.289, f32[12,544]{1,0:T(8,128)S(1)} %get-tuple-element.288, f32[12,544,544]{1,2,0:T(8,128)} %get-tuple-element.284, f32[12,544]{1,0:T(8,128)S(1)} %get-tuple-element.283), kind=kLoop, calls=%fused_computation.6 | loop fusion | flops 14204928 | bytes 35564544 | tf_op jit(solution)/shard_map/convert_element_type | solution.py:154
  350.0 3.7 fusion.35
  353.7 2.7 fusion.34
  356.7 9.1 %fusion.31 = bf16[544,1,12,64]{0,3,2,1:T(8,128)(2,1)S(1)} fusion(bf16[544,12,64]{0,2,1:T(8,128)(2,1)} %bitcast.151, f32[12,544,544]{1,2,0:T(8,128)} %get-tuple-element.284, f32[12,544]{1,0:T(8,128)S(1)} %get-tuple-element.283), kind=kOutput, calls=%fused_computation.76 | convolution fusion | flops 462077952 | bytes 15902208 | tf_op jit(solution)/shard_map/hqk,qhd->khd/dot_general | solution.py:158
  368.7 3.2 convolution_convert_fusion
  371.9 3.7 copy.241
  375.7 6.5 multiply_convert_fusion.1
  384.0 5.6 convolution_convert_fusion.1
  391.2 7.8 convolution_convert_fusion.2
  399.2 2.0 copy.268
  401.3 24.6 %reduce-scatter.23.cloned.1.call-done = bf16[768,3,192]{0,2,1:T(8,128)(2,1)} async-done(((bf16[768,3,768]{0,2,1:T(8,128)(2,1)}), bf16[768,3,192]{0,2,1:T(8,128)(2,1)}) %reduce-scatter.23.cloned.1.call-update) | async-done | bytes 884752 | tf_op jit(solution)/shard_map/reduce_scatter | solution.py:198
  425.9 2.2 copy.274
  428.6 85.0 %reduce-scatter.33.cloned.1.call-done = bf16[3072,192]{0,1:T(8,128)(2,1)} async-done(((bf16[3072,768]{0,1:T(8,128)(2,1)}), bf16[3072,192]{0,1:T(8,128)(2,1)}) %reduce-scatter.33.cloned.1.call-update) | async-done | bytes 1179664 | tf_op jit(solution)/shard_map/reduce_scatter | solution.py:198
  519.7 6.9 add_convert_fusion.4
  528.0 4.2 all-to-all-start.1
  532.4 6.6 multiply_reduce_fusion.3
  539.0 25.5 %reduce-scatter.27.cloned.1.call-done = bf16[768,768]{1,0:T(8,128)(2,1)} async-done(((bf16[768,3072]{1,0:T(8,128)(2,1)}), bf16[768,768]{1,0:T(8,128)(2,1)}) %reduce-scatter.27.cloned.1.call-update) | async-done | bytes 1179664 | tf_op jit(solution)/shard_map/reduce_scatter | solution.py:198
  564.8 3.0 add_convert_fusion.3
  567.8 2.2 copy.239
  570.1 4.6 all-to-all-start.3
  578.1 5.2 fusion.3
  583.3 4.6 reduce-scatter.41.cloned.1.call-done
  588.0 2.6 fusion.110
  590.6 8.5 %all-to-all-done.3 = bf16[4,544,192]{1,2,0:T(8,128)(2,1)S(1)} async-done(((bf16[4,544,192]{1,2,0:T(8,128)(2,1)}), bf16[4,544,192]{1,2,0:T(8,128)(2,1)S(1)}, u32[]{:S(2)}, u32[]{:S(2)}) %all-to-all-start.3) | async-done | bytes 835616 | tf_op jit(solution)/shard_map/all_to_all | solution.py:226
  600.5 15.8 %reduce-scatter.37.cloned.1.call-done = bf16[192,576]{1,0:T(8,128)(2,1)} async-done(((bf16[768,576]{1,0:T(8,128)(2,1)}), bf16[192,576]{1,0:T(8,128)(2,1)}) %reduce-scatter.37.cloned.1.call-update) | async-done | bytes 221200
  616.3 5.2 fusion.1
  621.5 21.8 %reduce-scatter.35.cloned.1.call-done = bf16[768,192]{0,1:T(8,128)(2,1)} async-done(((bf16[3072,192]{0,1:T(8,128)(2,1)}), bf16[768,192]{0,1:T(8,128)(2,1)}) %reduce-scatter.35.cloned.1.call-update) | async-done | bytes 294928 | tf_op jit(solution)/shard_map/reduce_scatter | solution.py:198
  646.8 3.0 copy.250
  651.5 23.2 %reduce-scatter.29.cloned.1.call-done = bf16[192,768]{1,0:T(8,128)(2,1)} async-done(((bf16[768,768]{1,0:T(8,128)(2,1)}), bf16[192,768]{1,0:T(8,128)(2,1)}) %reduce-scatter.29.cloned.1.call-update) | async-done | bytes 294928 | tf_op jit(solution)/shard_map/reduce_scatter | solution.py:198
  675.0 10.5 %reduce-scatter.43.cloned.1.call-done = bf16[96,192]{1,0:T(8,128)(2,1)} async-done(((bf16[192,192]{1,0:T(8,128)(2,1)}), bf16[96,192]{1,0:T(8,128)(2,1)}) %reduce-scatter.43.cloned.1.call-update) | async-done | bytes 36880
  687.0 12.1 %reduce-scatter.39.cloned.1.call-done = bf16[96,576]{1,0:T(8,128)(2,1)} async-done(((bf16[192,576]{1,0:T(8,128)(2,1)}), bf16[96,576]{1,0:T(8,128)(2,1)}) %reduce-scatter.39.cloned.1.call-update) | async-done | bytes 110608
  702.1 12.2 %reduce-scatter.45.cloned.1.call-done = bf16[384,192]{1,0:T(8,128)(2,1)} async-done(((bf16[768,192]{1,0:T(8,128)(2,1)}), bf16[384,192]{1,0:T(8,128)(2,1)}) %reduce-scatter.45.cloned.1.call-update) | async-done | bytes 147472
  716.1 12.5 %reduce-scatter.31.cloned.1.call-done = bf16[96,768]{1,0:T(8,128)(2,1)} async-done(((bf16[192,768]{1,0:T(8,128)(2,1)}), bf16[96,768]{1,0:T(8,128)(2,1)}) %reduce-scatter.31.cloned.1.call-update) | async-done | bytes 147472 | tf_op jit(solution)/shard_map/reduce_scatter | solution.py:198
  731.5 3.0 copy.251
  734.5 40.1 %all-reduce = (f32[]{:T(128)}, f32[1536]{0:T(1024)S(1)}, f32[7680]{0:T(1024)S(1)}) all-reduce(f32[]{:T(128)S(6)} %add.525, f32[1536]{0:T(1024)S(1)} %copy-done.50, f32[7680]{0:T(1024)S(1)} %copy-done.49), channel_id=1, replica_groups=mesh['dp'=2,'row'=4,'col'=4] {'dp','row','col'}, use_global_device_ids=true, to_apply=%region_33.34 | all-reduce | flops 9217 | bytes 73736 | tf_op jit(solution)/shard_map/psum | solution.py:248
  788.9 2.1 fusion.100
  (320 shorter events, 88.1 us)
Async XLA Ops:
  7.2 81.3 %all-gather.11.cloned.1.call-start = ((), (), s32[]{:S(2)}) async-start(), calls=%async_computation.18 | async-start | bytes 1474560 | tf_op jit(solution)/shard_map/all_gather | solution.py:192
  15.8 155.5 %all-gather.15.cloned.1.call-start = ((), (), s32[]{:S(2)}) async-start(), calls=%async_computation.20 | async-start | bytes 1474560 | tf_op jit(solution)/shard_map/all_gather | solution.py:192
  22.8 52.6 %copy-start.24 = (f32[96,192]{1,0:T(8,128)S(1)}, f32[96,192]{1,0:T(8,128)}, u32[]{:S(2)}) copy-start(f32[96,192]{1,0:T(8,128)} %param.25) | copy-start | bytes 221188
  22.8 173.4 %all-gather.7.cloned.1.call-start = ((), (), s32[]{:S(2)}) async-start(), calls=%async_computation.16 | async-start | bytes 4423680 | tf_op jit(solution)/shard_map/all_gather | solution.py:192
  30.3 57.2 %copy-start.65 = (s32[2070]{0:T(1024)S(1)}, s32[2070]{0:T(1024)}, u32[]{:S(2)}) copy-start(s32[2070]{0:T(1024)} %param.23) | copy-start | bytes 24844
  30.3 57.9 %copy-start.13 = (bf16[1035,1,384]{2,0,1:T(8,128)(2,1)S(1)}, bf16[1035,1,384]{2,0,1:T(8,128)(2,1)}, u32[]{:S(2)}) copy-start(bf16[1035,1,384]{2,0,1:T(8,128)(2,1)} %param.21) | copy-start | bytes 2384644
  75.3 168.8 %all-gather.9.cloned.1.call-start = ((), (), s32[]{:S(2)}) async-start(), calls=%async_computation.17 | async-start | bytes 1474560 | tf_op jit(solution)/shard_map/all_gather | solution.py:192
  87.5 161.4 %all-gather.13.cloned.1.call-start = ((), (), s32[]{:S(2)}) async-start(), calls=%async_computation.19 | async-start | bytes 5898240 | tf_op jit(solution)/shard_map/all_gather | solution.py:192
  87.5 1.0 collective-permute-start
  112.0 15.9 %copy-start.56 = (s32[2176]{0:T(1024)}, s32[2176]{0:T(1024)S(1)}, u32[]{:S(2)}) copy-start(s32[2176]{0:T(1024)S(1)} %fusion.55) | copy-start | bytes 26116
  116.3 11.4 %copy-start.14 = (bf16[1035,1,384]{2,0,1:T(8,128)(2,1)S(1)}, bf16[1035,1,384]{2,0,1:T(8,128)(2,1)}, u32[]{:S(2)}) copy-start(bf16[1035,1,384]{2,0,1:T(8,128)(2,1)} %param.22) | copy-start | bytes 2384644
  118.3 48.1 %all-to-all-start = ((bf16[4,544,192]{1,2,0:T(8,128)(2,1)}), bf16[4,544,192]{1,2,0:T(8,128)(2,1)S(1)}, u32[]{:S(2)}, u32[]{:S(2)}) async-start(bf16[4,544,192]{1,2,0:T(8,128)(2,1)} %copy.223), calls=%async_computation | async-start | bytes 1966080 | tf_op jit(solution)/shard_map/all_to_all | solution.py:221
  132.1 37.9 %copy-start.44 = (f32[1536]{0:T(1024)S(1)}, f32[1536]{0:T(1024)}, u32[]{:S(2)}) copy-start(f32[1536]{0:T(1024)} %param.28) | copy-start | bytes 18436
  132.2 38.0 %copy-start.33 = (f32[7680]{0:T(1024)S(1)}, f32[7680]{0:T(1024)}, u32[]{:S(2)}) copy-start(f32[7680]{0:T(1024)} %param.29) | copy-start | bytes 92164
  166.4 28.1 %all-to-all-start.2 = ((bf16[4,544,192]{1,2,0:T(8,128)(2,1)}), bf16[4,544,192]{1,2,0:T(8,128)(2,1)S(1)}, u32[]{:S(2)}, u32[]{:S(2)}) async-start(bf16[4,544,192]{1,2,0:T(8,128)(2,1)} %copy.232), calls=%async_computation.2 | async-start | bytes 1966080 | tf_op jit(solution)/shard_map/all_to_all | solution.py:221
  170.0 121.2 %all-gather.17.cloned.1.call-start = ((), (), s32[]{:S(2)}) async-start(), calls=%async_computation.21 | async-start | bytes 5898240 | tf_op jit(solution)/shard_map/all_gather | solution.py:192
  170.1 147.2 %copy-start.54 = (f32[768]{0:T(1024)}, f32[768]{0:T(1024)S(1)}, u32[]{:S(2)}) copy-start(f32[768]{0:T(1024)S(1)} %get-tuple-element.251) | copy-start | bytes 9220
  170.8 78.2 %copy-start.60 = (f32[768]{0:T(1024)}, f32[768]{0:T(1024)S(1)}, u32[]{:S(2)}) copy-start(f32[768]{0:T(1024)S(1)} %get-tuple-element.244) | copy-start | bytes 9220
  171.3 24.5 %copy-start.38 = (f32[544]{0:T(1024)}, f32[544]{0:T(1024)S(1)}, u32[]{:S(2)}) copy-start(f32[544]{0:T(1024)S(1)} %broadcast_multiply_fusion.5) | copy-start | bytes 6532
  171.4 227.8 %reduce-scatter.25.cloned.1.call-start = ((), (), s32[]{:S(2)}) async-start(), calls=%async_computation.23 | async-start | bytes 1474560 | tf_op jit(solution)/shard_map/reduce_scatter | solution.py:198
  248.9 68.4 %copy-start.52 = (f32[544]{0:T(1024)}, f32[544]{0:T(1024)S(1)}, u32[]{:S(2)}) copy-start(f32[544]{0:T(1024)S(1)} %add_rsqrt_fusion) | copy-start | bytes 6532
  291.2 22.4 %copy-start.6 = (f32[544,768]{1,0:T(8,128)S(1)}, f32[544,768]{1,0:T(8,128)}, u32[]{:S(2)}) copy-start(f32[544,768]{1,0:T(8,128)} %copy-done.5) | copy-start | bytes 5013508
  291.2 22.4 %copy-start.64 = (bf16[768,3072]{1,0:T(8,128)(2,1)S(1)}, bf16[768,3072]{1,0:T(8,128)(2,1)}, u32[]{:S(2)}) copy-start(bf16[768,3072]{1,0:T(8,128)(2,1)} %all-gather.13.cloned.1.call-done) | copy-start | bytes 14155780
  356.4 9.4 %copy-start.8 = (bf16[544,1,12,64]{0,3,2,1:T(8,128)(2,1)S(1)}, bf16[544,1,12,64]{0,3,2,1:T(8,128)(2,1)}, u32[]{:S(2)}) copy-start(bf16[544,1,12,64]{0,3,2,1:T(8,128)(2,1)} %fusion.35) | copy-start | bytes 2506756
  356.4 9.4 %copy-start.9 = (bf16[544,1,12,64]{0,3,2,1:T(8,128)(2,1)S(1)}, bf16[544,1,12,64]{0,3,2,1:T(8,128)(2,1)}, u32[]{:S(2)}) copy-start(bf16[544,1,12,64]{0,3,2,1:T(8,128)(2,1)} %fusion.34) | copy-start | bytes 2506756
  356.4 69.5 %reduce-scatter.23.cloned.1.call-start = ((), (), s32[]{:S(2)}) async-start(), calls=%async_computation.22 | async-start | bytes 4423680 | tf_op jit(solution)/shard_map/reduce_scatter | solution.py:198
  375.6 138.0 %reduce-scatter.33.cloned.1.call-start = ((), (), s32[]{:S(2)}) async-start(), calls=%async_computation.27 | async-start | bytes 5898240 | tf_op jit(solution)/shard_map/reduce_scatter | solution.py:198
  389.6 174.9 %reduce-scatter.27.cloned.1.call-start = ((), (), s32[]{:S(2)}) async-start(), calls=%async_computation.24 | async-start | bytes 5898240 | tf_op jit(solution)/shard_map/reduce_scatter | solution.py:198
  399.1 114.5 %copy-start.25 = (f32[96,192]{1,0:T(8,128)S(1)}, f32[96,192]{1,0:T(8,128)}, u32[]{:S(2)}) copy-start(f32[96,192]{1,0:T(8,128)} %param.25) | copy-start | bytes 221188
  399.1 115.3 %copy-start.20 = (f32[96,3,192]{2,0,1:T(8,128)S(1)}, f32[96,3,192]{2,0,1:T(8,128)}, u32[]{:S(2)}) copy-start(f32[96,3,192]{2,0,1:T(8,128)} %param.24) | copy-start | bytes 663556
  399.1 116.1 %copy-start.35 = (f32[96,192]{1,0:T(8,128)S(1)}, f32[96,192]{1,0:T(8,128)}, u32[]{:S(2)}) copy-start(f32[96,192]{1,0:T(8,128)} %param.32) | copy-start | bytes 221188
  399.1 116.9 %copy-start.36 = (f32[96,192]{1,0:T(8,128)S(1)}, f32[96,192]{1,0:T(8,128)}, u32[]{:S(2)}) copy-start(f32[96,192]{1,0:T(8,128)} %param.33) | copy-start | bytes 221188
  399.1 117.6 %copy-start.32 = (f32[96,3,192]{2,0,1:T(8,128)S(1)}, f32[96,3,192]{2,0,1:T(8,128)}, u32[]{:S(2)}) copy-start(f32[96,3,192]{2,0,1:T(8,128)} %param.30) | copy-start | bytes 663556
  399.2 188.8 %reduce-scatter.41.cloned.1.call-start = ((), (), s32[]{:S(2)}) async-start(), calls=%async_computation.31 | async-start | bytes 491520
  401.3 215.0 %reduce-scatter.37.cloned.1.call-start = ((), (), s32[]{:S(2)}) async-start(), calls=%async_computation.29 | async-start | bytes 1228800
  425.9 93.8 %copy-start.59 = (f32[768]{0:T(1024)S(1)}, f32[768]{0:T(1024)}, u32[]{:S(2)}) copy-start(f32[768]{0:T(1024)} %get-tuple-element.243) | copy-start | bytes 9220
  428.2 215.2 %reduce-scatter.35.cloned.1.call-start = ((), (), s32[]{:S(2)}) async-start(), calls=%async_computation.28 | async-start | bytes 1474560 | tf_op jit(solution)/shard_map/reduce_scatter | solution.py:198
  528.0 42.0 %all-to-all-start.1 = ((bf16[4,544,192]{1,2,0:T(8,128)(2,1)}), bf16[4,544,192]{1,2,0:T(8,128)(2,1)}, u32[]{:S(2)}, u32[]{:S(2)}) async-start(bf16[4,544,192]{1,2,0:T(8,128)(2,1)} %bitcast.44), calls=%async_computation.1 | async-start | bytes 1966080 | tf_op jit(solution)/shard_map/all_to_all | solution.py:226
  532.3 32.3 %copy-start.37 = (f32[3,12,64]{2,1,0:T(8,128)S(1)}, f32[3,12,64]{2,1,0:T(8,128)}, u32[]{:S(2)}) copy-start(f32[3,12,64]{2,1,0:T(8,128)} %get-tuple-element.233) | copy-start | bytes 27652
  532.3 32.5 %copy-start.4 = (f32[544,768]{1,0:T(8,128)S(1)}, f32[544,768]{1,0:T(8,128)}, u32[]{:S(2)}) copy-start(f32[544,768]{1,0:T(8,128)} %copy-done.3) | copy-start | bytes 5013508
  532.3 142.4 %reduce-scatter.29.cloned.1.call-start = ((), (), s32[]{:S(2)}) async-start(), calls=%async_computation.25 | async-start | bytes 1474560 | tf_op jit(solution)/shard_map/reduce_scatter | solution.py:198
  564.8 10.1 %copy-start.63 = (f32[768]{0:T(1024)S(1)}, f32[768]{0:T(1024)}, u32[]{:S(2)}) copy-start(f32[768]{0:T(1024)} %get-tuple-element.191) | copy-start | bytes 9220
  564.8 10.7 %copy-start.58 = (f32[3072]{0:T(1024)S(1)}, f32[3072]{0:T(1024)}, u32[]{:S(2)}) copy-start(f32[3072]{0:T(1024)} %get-tuple-element.228) | copy-start | bytes 36868
  567.8 10.4 %copy-start.57 = (s32[2176]{0:T(1024)S(1)}, s32[2176]{0:T(1024)}, u32[]{:S(2)}) copy-start(s32[2176]{0:T(1024)} %copy-done.56) | copy-start | bytes 26116
  570.1 29.0 %all-to-all-start.3 = ((bf16[4,544,192]{1,2,0:T(8,128)(2,1)}), bf16[4,544,192]{1,2,0:T(8,128)(2,1)S(1)}, u32[]{:S(2)}, u32[]{:S(2)}) async-start(bf16[4,544,192]{1,2,0:T(8,128)(2,1)} %bitcast.61), calls=%async_computation.3 | async-start | bytes 1966080 | tf_op jit(solution)/shard_map/all_to_all | solution.py:226
  574.7 110.8 %reduce-scatter.43.cloned.1.call-start = ((), (), s32[]{:S(2)}) async-start(), calls=%async_computation.32 | async-start | bytes 147456
  587.9 111.1 %reduce-scatter.39.cloned.1.call-start = ((), (), s32[]{:S(2)}) async-start(), calls=%async_computation.30 | async-start | bytes 368640
  616.3 98.0 %reduce-scatter.45.cloned.1.call-start = ((), (), s32[]{:S(2)}) async-start(), calls=%async_computation.33 | async-start | bytes 589824
  645.2 83.4 %reduce-scatter.31.cloned.1.call-start = ((), (), s32[]{:S(2)}) async-start(), calls=%async_computation.26 | async-start | bytes 442368 | tf_op jit(solution)/shard_map/reduce_scatter | solution.py:198
  674.9 59.6 %copy-start.49 = (f32[7680]{0:T(1024)S(1)}, f32[7680]{0:T(1024)}, u32[]{:S(2)}) copy-start(f32[7680]{0:T(1024)} %copy-done.48) | copy-start | bytes 92164
  674.9 59.6 %copy-start.50 = (f32[1536]{0:T(1024)S(1)}, f32[1536]{0:T(1024)}, u32[]{:S(2)}) copy-start(f32[1536]{0:T(1024)} %pad_maximum_fusion.2) | copy-start | bytes 18436
  674.9 102.9 %copy-start.26 = (f32[96,192]{0,1:T(8,128)S(1)}, f32[96,192]{0,1:T(8,128)}, u32[]{:S(2)}) copy-start(f32[96,192]{0,1:T(8,128)} %copy.249) | copy-start | bytes 221188
  674.9 102.9 %copy-start.27 = (f32[96,192]{0,1:T(8,128)S(1)}, f32[96,192]{0,1:T(8,128)}, u32[]{:S(2)}) copy-start(f32[96,192]{0,1:T(8,128)} %copy.246) | copy-start | bytes 221188
  674.9 102.9 %copy-start.28 = (f32[96,192]{0,1:T(8,128)S(1)}, f32[96,192]{0,1:T(8,128)}, u32[]{:S(2)}) copy-start(f32[96,192]{0,1:T(8,128)} %copy.247) | copy-start | bytes 221188
  674.9 104.4 %copy-start.17 = (f32[96,3,192]{0,2,1:T(8,128)S(1)}, f32[96,3,192]{0,2,1:T(8,128)}, u32[]{:S(2)}) copy-start(f32[96,3,192]{0,2,1:T(8,128)} %copy.245) | copy-start | bytes 663556
  674.9 104.4 %copy-start.18 = (f32[96,3,192]{0,2,1:T(8,128)S(1)}, f32[96,3,192]{0,2,1:T(8,128)}, u32[]{:S(2)}) copy-start(f32[96,3,192]{0,2,1:T(8,128)} %copy.242) | copy-start | bytes 663556
  674.9 104.4 %copy-start.19 = (f32[96,3,192]{0,2,1:T(8,128)S(1)}, f32[96,3,192]{0,2,1:T(8,128)}, u32[]{:S(2)}) copy-start(f32[96,3,192]{0,2,1:T(8,128)} %copy.243) | copy-start | bytes 663556
  734.5 53.0 %copy-start.34 = (f32[7680]{0:T(1024)S(1)}, f32[7680]{0:T(1024)}, u32[]{:S(2)}) copy-start(f32[7680]{0:T(1024)} %param.29) | copy-start | bytes 92164
  734.5 54.4 %copy-start.15 = (f32[384,192]{0,1:T(8,128)S(1)}, f32[384,192]{0,1:T(8,128)}, u32[]{:S(2)}) copy-start(f32[384,192]{0,1:T(8,128)} %param.27) | copy-start | bytes 884740
  778.6 10.3 %copy-start.29 = (f32[384,192]{0,1:T(8,128)S(1)}, f32[384,192]{0,1:T(8,128)}, u32[]{:S(2)}) copy-start(f32[384,192]{0,1:T(8,128)} %param.37) | copy-start | bytes 884740
  779.3 11.7 %copy-start.16 = (f32[96,768]{1,0:T(8,128)S(1)}, f32[96,768]{1,0:T(8,128)}, u32[]{:S(2)}) copy-start(f32[96,768]{1,0:T(8,128)} %param.26) | copy-start | bytes 884740
  779.3 11.7 %copy-start.23 = (bf16[96,768]{1,0:T(8,128)(2,1)S(1)}, bf16[96,768]{1,0:T(8,128)(2,1)}, u32[]{:S(2)}) copy-start(bf16[96,768]{1,0:T(8,128)(2,1)} %reduce-scatter.31.cloned.1.call-done) | copy-start | bytes 442372
  779.6 11.4 %copy-start.30 = (f32[96,768]{1,0:T(8,128)S(1)}, f32[96,768]{1,0:T(8,128)}, u32[]{:S(2)}) copy-start(f32[96,768]{1,0:T(8,128)} %param.35) | copy-start | bytes 884740
  779.6 11.4 %copy-start.31 = (f32[96,768]{1,0:T(8,128)S(1)}, f32[96,768]{1,0:T(8,128)}, u32[]{:S(2)}) copy-start(f32[96,768]{1,0:T(8,128)} %param.34) | copy-start | bytes 884740
  (27 other events, 106.9 us)
Sparse Core Ops, SparseCore 0:
  15.9 45.6 all-gather.10
  63.3 17.1 all-gather.14
  82.0 30.7 all-gather.6
  114.8 48.5 all-gather.8
  164.8 35.4 all-gather.12
  201.7 89.4 all-gather.16
  356.5 27.6 reduce-scatter.24
  386.7 39.1 reduce-scatter.22
  428.3 85.2 reduce-scatter.32
  516.1 48.3 reduce-scatter.26
  567.0 20.8 reduce-scatter.40
  590.1 26.1 reduce-scatter.36
  619.0 24.2 reduce-scatter.34
  645.5 29.1 reduce-scatter.28
  676.8 8.6 reduce-scatter.42
  687.6 11.4 reduce-scatter.38
  701.2 13.1 reduce-scatter.44
  716.5 12.0 reduce-scatter.30

commit v2 on v1

--- a/solution.py
+++ b/solution.py
@@ -1,6 +1,8 @@
 import jax
 import jax.numpy as jnp
 from jax import lax
+from jax.experimental import pallas as pl
+from jax.experimental.pallas import tpu as pltpu
 from jax.sharding import PartitionSpec as P
 
 HEADS = 12
@@ -90,6 +92,983 @@
     for number, (first, length, _, _) in enumerate(slot_segments(kind)):
         crop = jnp.where((slot >= first) & (slot < first + length), number, crop)
     return crop
+
+
+MESH = pl.DeviceIdType.MESH
+HALF = 64
+QW = 640
+TOK = 1040
+CHUNK = 32
+WQ, WO, W1, W2 = 0, 1, 2, 3
+VMEM_LIMIT = 60 * 2**20
+
+
+def mm(a, b):
+    return lax.dot_general(a, b, (((1,), (0,)), ((), ())), preferred_element_type=F32)
+
+
+def mm_nt(a, b):
+    return lax.dot_general(a, b, (((1,), (1,)), ((), ())), preferred_element_type=F32)
+
+
+def mm_tn(a, b):
+    return lax.dot_general(a, b, (((0,), (0,)), ((), ())), preferred_element_type=F32)
+
+
+class Place:
+    def __init__(self):
+        self.y = lax.axis_index("dp")
+        self.z = lax.axis_index("row")
+        self.c = lax.axis_index("col")
+        self.core = lax.rem(self.c, 2)
+        self.x = lax.div(self.c, 2)
+        self.cx = lax.rem(self.c + 2, 4)
+        self.cs = self.c + 1 - 2 * self.core
+        self.xn = (self.y, self.z, self.cx)
+        self.yn = (1 - self.y, self.z, self.c)
+        self.cn = (self.y, self.z, self.cs)
+        self.low = self.z < 2
+        self.mid = jnp.logical_or(self.z == 1, self.z == 2)
+        self.step = jnp.where(self.low, 1, -1)
+
+    def zth(self, z):
+        return (self.y, z, self.c)
+
+    def other(self, j):
+        return lax.rem(self.z + self.step * j + 4, 4)
+
+    def enter(self):
+        barrier = pltpu.get_barrier_semaphore()
+        peers = [self.zth(lax.rem(self.z + k, 4)) for k in (1, 2, 3)] + [self.xn, self.yn, self.cn]
+        for peer in peers:
+            pl.semaphore_signal(barrier, inc=1, device_id=peer, device_id_type=MESH)
+        pl.semaphore_wait(barrier, len(peers))
+
+
+def shard_of(refs, p, c, s, y):
+    ref = refs[p]
+    if p == WO:
+        return ref.at[s, c, pl.ds(pl.multiple_of(y * 96, 32), 96), :]
+    if p == W2:
+        return ref.at[c, s, :, pl.ds(pl.multiple_of(y * 384, 128), 384)]
+    return ref.at[c, s, y]
+
+
+def group_of(refs, p, c, y):
+    ref = refs[p]
+    if p == WO:
+        return ref.at[:, c, pl.ds(pl.multiple_of(y * 96, 32), 96), :]
+    if p == W2:
+        return ref.at[c, :, :, pl.ds(pl.multiple_of(y * 384, 128), 384)]
+    return ref.at[c, :, y]
+
+
+class Sends:
+    def __init__(self):
+        self.left = []
+
+    def start(self, src, dst, send_sem, recv_sem, peer, when=None):
+        copy = pltpu.make_async_remote_copy(
+            src_ref=src, dst_ref=dst, send_sem=send_sem, recv_sem=recv_sem, device_id=peer, device_id_type=MESH
+        )
+        if when is None:
+            copy.start()
+        else:
+            pl.when(when)(copy.start)
+        self.left.append((copy, when))
+
+    def drain(self):
+        for copy, when in self.left:
+            if when is None:
+                copy.wait_send()
+            else:
+                pl.when(when)(copy.wait_send)
+        self.left = []
+
+
+def arrived(ref, sem, me):
+    pltpu.make_async_remote_copy(
+        src_ref=ref, dst_ref=ref, send_sem=sem, recv_sem=sem, device_id=me, device_id_type=MESH
+    ).wait_recv()
+
+
+class Gather:
+    def __init__(self, at, refs, sends, zs, zr, xs, xr, ys, yr, ds, dr, cs, cr):
+        self.at, self.refs, self.sends = at, refs, sends
+        self.zs, self.zr, self.xs, self.xr = zs, zr, xs, xr
+        self.ys, self.yr, self.ds, self.dr, self.cs, self.cr = ys, yr, ds, dr, cs, cr
+
+    def across(self, p, s):
+        at = self.at
+        own = shard_of(self.refs, p, at.c, s, at.y)
+        self.sends.start(own, own, self.xs.at[p, s], self.xr.at[p, s], at.xn)
+        self.sends.start(own, own, self.ys.at[p, s], self.yr.at[p, s], at.yn)
+
+    def own_across(self, p):
+        self.across(p, self.at.z)
+
+    def own_along(self, p):
+        at = self.at
+        own = shard_of(self.refs, p, at.c, at.z, at.y)
+        second = jnp.where(at.mid, at.z - at.step, at.z + 2 * at.step)
+        self.sends.start(own, own, self.zs.at[p, 0], self.zr.at[p, at.z], at.zth(at.z + at.step))
+        self.sends.start(own, own, self.zs.at[p, 1], self.zr.at[p, at.z], at.zth(second))
+
+    def to_core(self, p, g, c, y):
+        ref = group_of(self.refs, p, c, y)
+        self.sends.start(ref, ref, self.cs.at[p, g], self.cr.at[p, g], self.at.cn)
+
+    def along(self, p):
+        at = self.at
+        for j in (1, 2, 3):
+            s = at.other(j)
+            ref = shard_of(self.refs, p, at.c, s, at.y)
+            arrived(ref, self.zr.at[p, s], at.yn)
+            if j < 3:
+                self.sends.start(ref, ref, self.zs.at[p, 1 + j], self.zr.at[p, s], at.zth(at.z - at.step), when=at.mid)
+            self.across(p, s)
+        self.to_core(p, 0, at.c, at.y)
+
+    def cross(self, p):
+        at = self.at
+        for j in (0, 1, 2, 3):
+            s = at.other(j)
+            from_x = shard_of(self.refs, p, at.cx, s, at.y)
+            from_y = shard_of(self.refs, p, at.c, s, 1 - at.y)
+            arrived(from_x, self.xr.at[p, s], at.yn)
+            arrived(from_y, self.yr.at[p, s], at.yn)
+            if j < 2:
+                self.sends.start(from_x, from_x, self.ds.at[p, j], self.dr.at[p, s], at.yn)
+            else:
+                self.sends.start(from_y, from_y, self.ds.at[p, j], self.dr.at[p, s], at.xn)
+        self.to_core(p, 1, at.cx, at.y)
+        self.to_core(p, 2, at.c, 1 - at.y)
+
+    def corner(self, p):
+        at = self.at
+        for j in (0, 1, 2, 3):
+            s = at.other(j)
+            arrived(shard_of(self.refs, p, at.cx, s, 1 - at.y), self.dr.at[p, s], at.yn)
+        self.to_core(p, 3, at.cx, 1 - at.y)
+
+    def ready(self, p):
+        at = self.at
+        other_x = at.cs + 2 - 4 * at.x
+        for g, (c, y) in enumerate(((at.cs, at.y), (other_x, at.y), (at.cs, 1 - at.y), (other_x, 1 - at.y))):
+            arrived(group_of(self.refs, p, c, y), self.cr.at[p, g], at.yn)
+
+
+def exchange_start(at, sends, blocks, landing, send_sems, recv_sems):
+    for k in (1, 2, 3):
+        to = lax.rem(at.z + k, 4)
+        sends.start(blocks.at[to], landing.at[at.z], send_sems.at[k - 1], recv_sems.at[at.z], at.zth(to))
+
+
+def exchange_wait(at, landing, recv_sems):
+    for k in (1, 2, 3):
+        s = lax.rem(at.z + k, 4)
+        arrived(landing.at[s], recv_sems.at[s], at.yn)
+
+
+def row_stats(value):
+    centre = jnp.sum(value, axis=1, keepdims=True) * (1.0 / D)
+    centred = value - centre
+    spread = jnp.sum(centred * centred, axis=1, keepdims=True) * (1.0 / D)
+    inverse = lax.rsqrt(spread + NORM_EPS)
+    return centred * inverse, inverse
+
+
+def chunks(body):
+    def step(i, carry):
+        body(pl.ds(pl.multiple_of(i * CHUNK, CHUNK), CHUNK))
+        return carry
+
+    lax.fori_loop(0, SLOTS // CHUNK, step, 0)
+
+
+def loop(count, body):
+    def step(i, carry):
+        body(i)
+        return carry
+
+    lax.fori_loop(0, count, step, 0)
+
+
+def lane_low(rows):
+    return lax.broadcasted_iota(jnp.int32, (rows, 2 * HALF), 1) < HALF
+
+
+def swap_halves(value):
+    return jnp.concatenate([value[:, HALF:], value[:, :HALF]], axis=1)
+
+
+def segments(kind):
+    if kind == 0:
+        return ((0, BIG_SLOTS, True, 0), (BIG_SLOTS, BIG_SLOTS, True, 1), (2 * BIG_SLOTS, 128, False, 0))
+    return ((0, BIG_SLOTS, True, 0),) + tuple((BIG_SLOTS + t * TRIO_SLOTS, TRIO_SLOTS, False, t) for t in range(3))
+
+
+def key_mask(size, is_big):
+    key = lax.broadcasted_iota(jnp.int32, (size, size), 1)
+    if is_big:
+        return key < BIG_CROP
+    query = lax.broadcasted_iota(jnp.int32, (size, size), 0)
+
+    def crop(v):
+        return (v >= SMALL_CROP).astype(jnp.int32) + (v >= 2 * SMALL_CROP).astype(jnp.int32) + (v >= TRIO).astype(jnp.int32)
+
+    return jnp.logical_and(crop(query) == crop(key), key < TRIO)
+
+
+def attend_segment(c, segment, qkv, mixed, pbig, ptrio):
+    first, size, is_big, index = segment
+    rows = pl.ds(first, size)
+    q01 = qkv[c, rows, 0:128]
+    k01 = qkv[c, rows, 128:256]
+    v01 = qkv[c, rows, 256:384]
+    qk2 = qkv[c, rows, 384:512]
+    v2 = qkv[c, rows, 512:640]
+    low = lane_low(size)
+    none = jnp.zeros((size, 128), BF)
+    mask = key_mask(size, is_big)
+    outs = []
+    for h, (q, k, v) in enumerate((
+        (jnp.where(low, q01, none), k01, v01),
+        (jnp.where(low, none, q01), k01, v01),
+        (jnp.where(low, qk2, none), swap_halves(qk2), v2),
+    )):
+        scores = jnp.where(mask, mm_nt(q, k) * HEAD_DIM**-0.5, MASKED)
+        weights = jnp.exp(scores - jnp.max(scores, axis=1, keepdims=True))
+        total = jnp.sum(weights, axis=1, keepdims=True)
+        weights = (weights * (1.0 / total)).astype(BF)
+        if is_big:
+            pbig[c, h, index] = weights
+        else:
+            ptrio[c, h, index, 0:size, 0:size] = weights
+        outs.append(mm(weights, v))
+    mixed[rows, pl.ds(pl.multiple_of(c * 256, 256), 128)] = jnp.where(low, outs[0], outs[1]).astype(BF)
+    mixed[rows, pl.ds(pl.multiple_of(c * 256 + 128, 128), 128)] = outs[2].astype(BF)
+
+
+def attend(at, c, qkv, mixed, pbig, ptrio):
+    for kind in (0, 1):
+
+        @pl.when(at.low if kind == 0 else jnp.logical_not(at.low))
+        def _():
+            for segment in segments(kind):
+                attend_segment(c, segment, qkv, mixed, pbig, ptrio)
+
+
+def transpose_into(dst, src, tiles):
+    def body(j):
+        lanes = pl.ds(pl.multiple_of(j * 128, 128), 128)
+        dst[lanes, :] = src[:, lanes].T
+
+    loop(tiles, body)
+
+
+def forward_kernel(
+    x_in, g_in, place, wq_in, wo_in, w1_in, w2_in, gains, biases, qkv_bias,
+    wq_h, wo_h, w1_h, w2_h, x_h, mid_h, a1t_h, a2t_h, mixt_h, qkv_h, pbig_h, ptrio_h, act_h, slope_h, cot_h, cott_h, out_h,
+    wq, wo, w1, w2, tok, send_x, send_g, land_x, land_g, x, mid, midb, a1, a1t, a2t, mixed, mixt, qkv, pbig, ptrio,
+    act, slope, cot, cott, out,
+    zs, zr, xs, xr, ys, yr, ds, dr, cs, cr, exs, exr, egs, egr, hs,
+):
+    at = Place()
+    refs = (wq, wo, w1, w2)
+    sends = Sends()
+    gather = Gather(at, refs, sends, zs, zr, xs, xr, ys, yr, ds, dr, cs, cr)
+    at.enter()
+    stores = []
+
+    def keep(src, dst):
+        copy = pltpu.make_async_copy(src, dst, hs.at[len(stores)])
+        copy.start()
+        stores.append(copy)
+
+    wq[at.c, at.z, at.y] = wq_in[...].astype(BF)
+    gather.own_along(WQ)
+    gather.own_across(WQ)
+    wo[at.z, at.c, pl.ds(pl.multiple_of(at.y * 96, 32), 96), :] = wo_in[...].astype(BF)
+    w1[at.c, at.z, at.y] = w1_in[...].astype(BF)
+    gather.own_across(WO)
+    gather.own_across(W1)
+    w2[at.c, at.z, :, pl.ds(pl.multiple_of(at.y * 384, 128), 384)] = w2_in[...].T.astype(BF)
+    gather.own_across(W2)
+
+    pairs = x_in.shape[0]
+    for n, ref in enumerate((x_in, g_in)):
+        for half in (0, 1):
+            tok[n, half * TOK + TOK - 16 : half * TOK + TOK, :] = jnp.zeros((16, 192), BF)
+            tok[n, half * TOK : half * TOK + pairs, :] = ref[:, half * 192 : half * 192 + 192]
+
+    def pick(r):
+        at_slot = place[pl.ds(pl.multiple_of(r * SLOTS, SLOTS), SLOTS), :]
+        one = (lax.broadcasted_iota(jnp.int32, (SLOTS, 2 * TOK), 1) == at_slot).astype(F32).astype(BF)
+        send_x[r] = mm(one, tok[0]).astype(BF)
+        send_g[r] = mm(one, tok[1]).astype(BF)
+
+    loop(4, pick)
+    exchange_start(at, sends, send_x, land_x, exs, exr)
+    land_x[at.z] = send_x[at.z]
+    land_g[at.z] = send_g[at.z]
+    gather.own_along(WO)
+    gather.own_along(W1)
+    gather.along(WQ)
+    wo[:, :, 192:256, :] = jnp.zeros((4, 4, 64, 192), BF)
+    exchange_wait(at, land_x, exr)
+
+    def norm_one(rows):
+        value = jnp.concatenate([land_x[r, rows, :] for r in range(4)], axis=1)
+        x[rows, :] = value
+        normed, _ = row_stats(value.astype(F32))
+        a1[rows, :] = (normed * gains[0:1, :] + biases[0:1, :]).astype(BF)
+
+    chunks(norm_one)
+    gather.along(WO)
+    gather.own_along(W2)
+    gather.cross(WQ)
+    transpose_into(a1t, a1, 6)
+    a1t[768:784, :] = jnp.ones((16, SLOTS), BF)
+    keep(a1t, a1t_h)
+    keep(x, x_h)
+    gather.along(W1)
+    exchange_start(at, sends, send_g, land_g, egs, egr)
+    gather.cross(WO)
+    gather.corner(WQ)
+    gather.ready(WQ)
+    wqv = wq.reshape(4, 768, QW)
+    keep(wqv, wq_h)
+
+    def project(c):
+        for n in range(0, QW, 256):
+            wide = min(256, QW - n)
+            qkv[c, :, n : n + wide] = (mm(a1[...], wqv[c, :, n : n + wide]) + qkv_bias[c, :, n : n + wide]).astype(BF)
+
+    loop(4, project)
+    keep(qkv, qkv_h)
+    gather.corner(WO)
+    gather.cross(W1)
+    loop(2, lambda c: attend(at, c, qkv, mixed, pbig, ptrio))
+    gather.along(W2)
+    loop(2, lambda c: attend(at, c + 2, qkv, mixed, pbig, ptrio))
+    keep(pbig, pbig_h)
+    keep(ptrio, ptrio_h)
+    gather.ready(WO)
+    gather.corner(W1)
+    wov = wo.reshape(4, 1024, 192)
+    keep(wov, wo_h)
+
+    def branch(z):
+        midb[z] = mm(mixed[...], wov[z])
+
+    loop(4, branch)
+
+    def norm_two(rows):
+        value = x[rows, :].astype(F32) + jnp.concatenate([midb[r, rows, :] for r in range(4)], axis=1) + biases[4:5, :]
+        mid[rows, :] = value
+        normed, _ = row_stats(value)
+        a1[rows, :] = (normed * gains[1:2, :] + biases[1:2, :]).astype(BF)
+
+    chunks(norm_two)
+    keep(mid, mid_h)
+    gather.cross(W2)
+    gather.ready(W1)
+    w1v = w1.reshape(4, 768, 768)
+    keep(w1v, w1_h)
+
+    def expand(c):
+        def tile(n):
+            lanes = pl.ds(pl.multiple_of(n * 256, 256), 256)
+            hidden = mm(a1[...], w1v[c, :, lanes]) + biases[pl.ds(6 + c, 1), lanes]
+            share = 0.5 + 0.5 * lax.erf(hidden * 0.7071067811865476)
+            bell = jnp.exp(hidden * hidden * -0.5) * 0.3989422804014327
+            act[c, :, lanes] = (hidden * share).astype(BF)
+            slope[c, :, lanes] = (share + hidden * bell).astype(BF)
+
+        loop(3, tile)
+
+    loop(4, expand)
+    keep(act, act_h)
+    keep(slope, slope_h)
+    gather.corner(W2)
+    transpose_into(a2t, a1, 6)
+    a2t[768:784, :] = jnp.ones((16, SLOTS), BF)
+    transpose_into(mixt, mixed, 8)
+    mixt[192:208, :] = jnp.ones((16, SLOTS), BF)
+    keep(a2t, a2t_h)
+    keep(mixt, mixt_h)
+    exchange_wait(at, land_g, egr)
+
+    def join(rows):
+        cot[rows, :] = jnp.concatenate([land_g[r, rows, :] for r in range(4)], axis=1)
+
+    chunks(join)
+    keep(cot, cot_h)
+    transpose_into(cott, cot, 6)
+    keep(cott, cott_h)
+    gather.ready(W2)
+    w2v = w2.reshape(4, 768, 768)
+    keep(w2v, w2_h)
+
+    def contract(n):
+        rows = pl.ds(pl.multiple_of(n * 256, 256), 256)
+        total = mm_nt(act[0], w2v[0, rows, :])
+        for c in (1, 2, 3):
+            total = total + mm_nt(act[c], w2v[c, rows, :])
+        midb2 = total + biases[5:6, rows] + mid[:, rows]
+        out[n] = midb2.astype(BF)
+
+    loop(3, contract)
+
+    def split(rows):
+        value = jnp.concatenate([out[n, rows, :] for n in range(3)], axis=1)
+        for r in range(4):
+            land_x[r, rows, :] = value[:, r * 192 : r * 192 + 192]
+
+    chunks(split)
+    keep(land_x, out_h)
+    sends.drain()
+    for copy in stores:
+        copy.wait()
+
+
+FORWARD_OUT = (
+    ((4, 768, QW), BF), ((4, 1024, 192), BF), ((4, 768, 768), BF), ((4, 768, 768), BF),
+    ((SLOTS, D), BF), ((SLOTS, D), F32), ((784, SLOTS), BF), ((784, SLOTS), BF), ((1024, SLOTS), BF),
+    ((4, SLOTS, QW), BF), ((4, 3, 2, BIG_SLOTS, BIG_SLOTS), BF), ((4, 3, 3, 128, 128), BF),
+    ((4, SLOTS, 768), BF), ((4, SLOTS, 768), BF), ((SLOTS, D), BF), ((D, SLOTS), BF), ((4, SLOTS, 192), BF),
+)
+
+
+def run_forward(*operands):
+    sem = pltpu.SemaphoreType.DMA
+    vmem = pltpu.VMEM
+    return pl.pallas_call(
+        forward_kernel,
+        out_shape=[jax.ShapeDtypeStruct(s, t) for s, t in FORWARD_OUT],
+        in_specs=[pl.BlockSpec(memory_space=vmem)] * len(operands),
+        out_specs=[pl.BlockSpec(memory_space=pl.ANY)] * len(FORWARD_OUT),
+        scratch_shapes=[
+            vmem((4, 4, 2, 96, QW), BF), vmem((4, 4, 256, 192), BF), vmem((4, 4, 2, 96, 768), BF), vmem((4, 4, 192, 768), BF),
+            vmem((2, 2 * TOK, 192), BF),
+            vmem((4, SLOTS, 192), BF), vmem((4, SLOTS, 192), BF), vmem((4, SLOTS, 192), BF), vmem((4, SLOTS, 192), BF),
+            vmem((SLOTS, D), BF), vmem((SLOTS, D), F32), vmem((4, SLOTS, 192), F32), vmem((SLOTS, D), BF),
+            vmem((784, SLOTS), BF), vmem((784, SLOTS), BF), vmem((SLOTS, 1024), BF), vmem((1024, SLOTS), BF),
+            vmem((4, SLOTS, QW), BF), vmem((4, 3, 2, BIG_SLOTS, BIG_SLOTS), BF), vmem((4, 3, 3, 128, 128), BF),
+            vmem((4, SLOTS, 768), BF), vmem((4, SLOTS, 768), BF), vmem((SLOTS, D), BF), vmem((D, SLOTS), BF),
+            vmem((3, SLOTS, 256), BF),
+            sem((4, 4)), sem((4, 4)), sem((4, 4)), sem((4, 4)), sem((4, 4)), sem((4, 4)), sem((4, 4)), sem((4, 4)),
+            sem((4, 4)), sem((4, 4)), sem((3,)), sem((4,)), sem((3,)), sem((4,)), sem((len(FORWARD_OUT),)),
+        ],
+        compiler_params=pltpu.CompilerParams(collective_id=0, has_side_effects=True, vmem_limit_bytes=VMEM_LIMIT),
+    )(*operands)
+
+
+class Reduce:
+    def __init__(self, at, sends, grads, pair, corner, cross, along, owned, small, sems):
+        self.at, self.sends = at, sends
+        self.grads, self.pair, self.corner, self.cross, self.along = grads, pair, corner, cross, along
+        self.owned, self.small = owned, small
+        self.ss, self.rs = sems
+
+    def start(self, p, n, src, dst, peer, arrival=None):
+        self.sends.start(src, dst, self.ss.at[p, n], self.rs.at[p, n if arrival is None else arrival], peer)
+
+    def pair_send(self, p):
+        at = self.at
+        for i in (0, 1):
+            c = 2 * i + 1 - at.core
+            self.start(p, i, self.grads[p].at[c], self.pair[p].at[i], at.cn)
+
+    def add(self, dst, src):
+        for s in range(dst.shape[0]):
+            dst[s] = dst[s] + src[s]
+
+    def pair_sum(self, p):
+        at, grads, pair = self.at, self.grads[p], self.pair[p]
+        for i in (0, 1):
+            arrived(pair.at[i], self.rs.at[p, i], at.yn)
+        far = 1 - at.x
+
+        def add(c, i, y):
+            def one(s):
+                grads[c, y, s] = grads[c, y, s] + pair[i, y, s]
+
+            loop(4, one)
+
+        add(at.cx, far, 1 - at.y)
+        self.start(p, 2, grads.at[at.cx, 1 - at.y, pl.ds(0, 2)], self.corner[p].at[0], at.xn)
+        self.start(p, 3, grads.at[at.cx, 1 - at.y, pl.ds(2, 2)], self.corner[p].at[1], at.yn)
+        add(at.cx, far, at.y)
+        self.start(p, 4, grads.at[at.cx, at.y, pl.ds(0, 2)], self.cross[p].at[0, pl.ds(0, 2)], at.xn)
+        add(at.c, at.x, 1 - at.y)
+        self.start(p, 5, grads.at[at.c, 1 - at.y, pl.ds(2, 2)], self.cross[p].at[1, pl.ds(2, 2)], at.yn)
+        add(at.c, at.x, at.y)
+
+    def corner_sum(self, p):
+        at, grads, corner = self.at, self.grads[p], self.corner[p]
+        arrived(corner.at[0], self.rs.at[p, 2], at.yn)
+
+        def one(s):
+            grads[at.c, 1 - at.y, s] = grads[at.c, 1 - at.y, s] + corner[0, s]
+
+        loop(2, one)
+        self.start(p, 6, grads.at[at.c, 1 - at.y, pl.ds(0, 2)], self.cross[p].at[1, pl.ds(0, 2)], at.yn)
+        arrived(corner.at[1], self.rs.at[p, 3], at.yn)
+
+        def two(s):
+            grads[at.cx, at.y, s + 2] = grads[at.cx, at.y, s + 2] + corner[1, s]
+
+        loop(2, two)
+        self.start(p, 7, grads.at[at.cx, at.y, pl.ds(2, 2)], self.cross[p].at[0, pl.ds(2, 2)], at.xn)
+
+    def cross_sum(self, p):
+        at, grads, cross = self.at, self.grads[p], self.cross[p]
+        for n, (i, half) in ((4, (0, 0)), (7, (0, 2)), (5, (1, 2)), (6, (1, 0))):
+            arrived(cross.at[i, pl.ds(half, 2)], self.rs.at[p, n], at.yn)
+
+        def one(s):
+            grads[at.c, at.y, s] = grads[at.c, at.y, s] + cross[0, s] + cross[1, s]
+
+        loop(4, one)
+        for k in (1, 2, 3):
+            to = lax.rem(at.z + k, 4)
+            self.start(p, 7 + k, grads.at[at.c, at.y, to], self.along[p].at[at.z], at.zth(to), arrival=8 + at.z)
+
+    def along_sum(self, p):
+        at, grads, along = self.at, self.grads[p], self.along[p]
+        for k in (1, 2, 3):
+            s = lax.rem(at.z + k, 4)
+            arrived(along.at[s], self.rs.at[p, 8 + s], at.yn)
+        total = grads[at.c, at.y, at.z].astype(F32)
+        for k in (1, 2, 3):
+            total = total + along[lax.rem(at.z + k, 4)].astype(F32)
+        self.owned[p][...] = total
+        wide = total.shape[1]
+        self.small[14:15, 0:wide] = self.small[14:15, 0:wide] + jnp.sum(total * total, axis=0, keepdims=True)
+
+
+def back_segment(c, slot, segment, qkv, weights_big, weights_trio, mixed, grads):
+    first, size, is_big, index = segment
+    rows = pl.ds(first, size)
+    q01 = qkv[c, rows, 0:128]
+    k01 = qkv[c, rows, 128:256]
+    v01 = qkv[c, rows, 256:384]
+    kq2 = swap_halves(qkv[c, rows, 384:512])
+    v2 = qkv[c, rows, 512:640]
+    g01 = mixed[rows, pl.ds(pl.multiple_of(c * 256, 256), 128)]
+    g2 = mixed[rows, pl.ds(pl.multiple_of(c * 256 + 128, 128), 128)]
+    low = lane_low(size)
+    none = jnp.zeros((size, 128), BF)
+    dq, dk, dv = [], [], []
+    for h, (g, gs, q, k, v) in enumerate((
+        (g01, jnp.where(low, g01, none), q01, k01, v01),
+        (g01, jnp.where(low, none, g01), q01, k01, v01),
+        (g2, g2, kq2, kq2, v2),
+    )):
+        if is_big:
+            weights = weights_big[slot, h, index]
+        else:
+            weights = weights_trio[slot, h, index, 0:size, 0:size]
+        wide = weights.astype(F32)
+        product = wide * mm_nt(gs, v)
+        scores = (product - wide * jnp.sum(product, axis=1, keepdims=True)).astype(BF)
+        dq.append(mm(scores, k))
+        dk.append(mm_tn(scores, q))
+        dv.append(mm_tn(weights, g))
+    scale = HEAD_DIM**-0.5
+    grads[c, rows, 0:128] = (jnp.where(low, dq[0], dq[1]) * scale).astype(BF)
+    grads[c, rows, 128:256] = (jnp.where(low, dk[0], dk[1]) * scale).astype(BF)
+    grads[c, rows, 256:384] = jnp.where(low, dv[0], dv[1]).astype(BF)
+    grads[c, rows, 384:512] = (jnp.where(low, dq[2], dk[2]) * scale).astype(BF)
+    grads[c, rows, 512:640] = dv[2].astype(BF)
+
+
+def backward_kernel(
+    wq_h, wo_h, w1_h, w2_h, x_h, mid_h, a1t_h, a2t_h, mixt_h, qkv_h, pbig_h, ptrio_h, act_h, slope_h, cot_h, cott_h, out_h,
+    gains,
+    own_q, own_o, own_1, own_2, total, land_out, land_in,
+    ring, wo, gq, go, g1, g2, pq, po, p1, p2, nq, no, n1, n2, rq, ro, r1, r2, lq, lo, l1, l2,
+    act, slope, cot, cott, a2t, a1t, mixt, mid, x, pbig, ptrio, gmix, grad, half, send, small, sums_of, line, plane,
+    ss, rs, hs, ring_s, p_s, ex_s, ex_r, in_s, in_r, line_s, line_r, plane_s, plane_r,
+):
+    at = Place()
+    sends = Sends()
+    reduce = Reduce(
+        at, sends, (gq, go, g1, g2), (pq, po, p1, p2), (nq, no, n1, n2), (rq, ro, r1, r2), (lq, lo, l1, l2),
+        (own_q, own_o, own_1, own_2), small, (ss, rs),
+    )
+    loads = {}
+
+    def load(name, src, dst):
+        copy = pltpu.make_async_copy(src, dst, hs.at[len(loads)])
+        copy.start()
+        loads[name] = copy
+
+    uses = [(w2_h, c) for c in range(4)] + [(w1_h, c) for c in range(4)] + [(wq_h, c) for c in range(4)]
+    ring_copies = {}
+
+    def ring_start(u):
+        if u < len(uses):
+            src, c = uses[u]
+            wide = src.shape[2]
+            copy = pltpu.make_async_copy(src.at[c], ring.at[u % 3, :, pl.ds(0, wide)], ring_s.at[u])
+            copy.start()
+            ring_copies[u] = copy
+
+    load("cott", cott_h, cott)
+    load("act", act_h, act)
+    for u in range(3):
+        ring_start(u)
+    load("cot", cot_h, cot)
+    load("slope", slope_h, slope)
+    load("a2t", a2t_h, a2t)
+    load("mid", mid_h, mid)
+    load("mixt", mixt_h, mixt)
+    load("wo", wo_h, wo)
+    load("a1t", a1t_h, a1t)
+    load("x", x_h, x)
+    at_enter(at)
+    keep_out = pltpu.make_async_copy(out_h.at[at.z], land_out.at[at.z], ex_s.at[3])
+    keep_out.start()
+    exchange_start(at, sends, out_h, land_out, ex_s, ex_r)
+    small[...] = jnp.zeros((16, D), F32)
+
+    def group(i):
+        return 2 * (i % 2) + (1 - at.core if i < 2 else at.core)
+
+    loads["cott"].wait()
+    loads["act"].wait()
+
+    def grad_fc2(c):
+        for n in range(3):
+            tile = mm(cott[...], act[c, :, n * 256 : n * 256 + 256]).astype(BF)
+            for z in range(4):
+                part = tile[z * 192 : z * 192 + 192]
+                if n == 0:
+                    g2[c, 0, z, :, 0:256] = part
+                elif n == 1:
+                    g2[c, 0, z, :, 256:384] = part[:, 0:128]
+                    g2[c, 1, z, :, 0:128] = part[:, 128:256]
+                else:
+                    g2[c, 1, z, :, 128:384] = part
+
+    loop(2, lambda i: grad_fc2(2 * i + 1 - at.core))
+    reduce.pair_send(W2)
+    loop(2, lambda i: grad_fc2(2 * i + at.core))
+    reduce.pair_sum(W2)
+    loads["cot"].wait()
+    loads["slope"].wait()
+
+    def grad_hidden(c):
+        ring_copies[c].wait()
+
+        def tile(n):
+            lanes = pl.ds(pl.multiple_of(n * 256, 256), 256)
+            slope[c, :, lanes] = (mm(cot[...], ring[c % 3, :, lanes]) * slope[c, :, lanes].astype(F32)).astype(BF)
+
+        loop(3, tile)
+        ring_start(c + 3)
+
+    grad_hidden(0)
+    grad_hidden(1)
+    grad_hidden(2)
+    grad_hidden(3)
+    reduce.corner_sum(W2)
+    loads["a2t"].wait()
+
+    def rows_to_shards(dst, c, lanes, tile):
+        for z in range(4):
+            for y in range(2):
+                first = (z * 2 + y) * 96
+                dst[c, y, z, :, lanes] = tile[first : first + 96].astype(BF)
+
+    def grad_fc1(c):
+        def tile(n):
+            lanes = pl.ds(pl.multiple_of(n * 256, 256), 256)
+            value = mm(a2t[...], slope[c, :, lanes])
+            rows_to_shards(g1, c, lanes, value)
+            sums_of[c, :, lanes] = value[768:769]
+
+        loop(3, tile)
+
+    loop(2, lambda i: grad_fc1(2 * i + 1 - at.core))
+    reduce.pair_send(W1)
+    loop(2, lambda i: grad_fc1(2 * i + at.core))
+    reduce.pair_sum(W1)
+    reduce.cross_sum(W2)
+
+    def back_through(u, c, left, wide):
+        ring_copies[u].wait()
+
+        def tile(n):
+            lanes = pl.ds(pl.multiple_of(n * 256, 256), 256)
+            part = mm_nt(left[c, :, 0:wide], ring[u % 3, lanes, 0:wide])
+            if c == 0:
+                grad[:, lanes] = part
+            else:
+                grad[:, lanes] = grad[:, lanes] + part
+
+        loop(3, tile)
+        ring_start(u + 3)
+
+    for c in range(4):
+        back_through(4 + c, c, slope, 768)
+    load("qkv", qkv_h, slope.at[:, :, pl.ds(0, QW)])
+    reduce.corner_sum(W1)
+    loads["mid"].wait()
+
+    def norm_two(i, sums):
+        rows = pl.ds(pl.multiple_of(i * CHUNK, CHUNK), CHUNK)
+        normed, inverse = row_stats(mid[rows, :])
+        upper = grad[rows, :]
+        weighted = upper * gains[1:2, :]
+        first = jnp.sum(weighted, axis=1, keepdims=True) * (1.0 / D)
+        second = jnp.sum(weighted * normed, axis=1, keepdims=True) * (1.0 / D)
+        straight = cot[rows, :].astype(F32)
+        value = straight + inverse * (weighted - first - normed * second)
+        mid[rows, :] = value
+        branch = value.astype(BF)
+        for r in range(4):
+            half[r, rows, :] = branch[:, r * 192 : r * 192 + 192]
+        parts = (upper * normed, upper, branch.astype(F32), straight)
+        return tuple(s + jnp.sum(v, axis=0, keepdims=True) for s, v in zip(sums, parts))
+
+    zero = jnp.zeros((1, D), F32)
+    sums = lax.fori_loop(0, SLOTS // CHUNK, norm_two, (zero,) * 4)
+    for r, value in zip((1, 3, 4, 5), sums):
+        small[r : r + 1, :] = value
+    loads["mixt"].wait()
+
+    def grad_out(z):
+        value = mm(mixt[...], half[z]).astype(BF)
+        for c in range(4):
+            for y in range(2):
+                go[c, y, z] = value[c * 256 + y * 96 : c * 256 + y * 96 + 96]
+
+    loop(4, grad_out)
+    reduce.pair_send(WO)
+    loads["wo"].wait()
+
+    def grad_mixed(c):
+        rows = pl.ds(pl.multiple_of(c * 256, 256), 256)
+        value = mm_nt(half[0], wo[0, rows, :])
+        for z in (1, 2, 3):
+            value = value + mm_nt(half[z], wo[z, rows, :])
+        gmix[:, rows] = value.astype(BF)
+
+    loop(4, grad_mixed)
+    reduce.pair_sum(WO)
+    loads["qkv"].wait()
+
+    def fetch(c, slot):
+        return (
+            pltpu.make_async_copy(pbig_h.at[c], pbig.at[slot], p_s.at[slot, 0]),
+            pltpu.make_async_copy(ptrio_h.at[c], ptrio.at[slot], p_s.at[slot, 1]),
+        )
+
+    for copy in fetch(0, 0):
+        copy.start()
+    for c in range(4):
+        for copy in fetch(c, c % 2):
+            copy.wait()
+        if c < 3:
+            for copy in fetch(c + 1, (c + 1) % 2):
+                copy.start()
+        for kind in (0, 1):
+
+            @pl.when(at.low if kind == 0 else jnp.logical_not(at.low))
+            def _():
+                for segment in segments(kind):
+                    back_segment(c, c % 2, segment, slope, pbig, ptrio, gmix, act)
+
+        if c == 0:
+            reduce.along_sum(W2)
+        elif c == 1:
+            reduce.cross_sum(W1)
+        elif c == 2:
+            reduce.corner_sum(WO)
+
+    loads["a1t"].wait()
+
+    def grad_q(c):
+        for n in range(0, QW, 256):
+            wide = min(256, QW - n)
+            value = mm(a1t[...], act[c, :, n : n + wide])
+            rows_to_shards(gq, c, slice(n, n + wide), value)
+            sums_of[4 + c, :, n : n + wide] = value[768:769]
+
+    loop(2, lambda i: grad_q(2 * i + 1 - at.core))
+    reduce.pair_send(WQ)
+    loop(2, lambda i: grad_q(2 * i + at.core))
+    reduce.pair_sum(WQ)
+    for c in range(4):
+        back_through(8 + c, c, act, QW)
+    reduce.along_sum(W1)
+    reduce.cross_sum(WO)
+    loads["x"].wait()
+
+    def norm_one(i, sums):
+        rows = pl.ds(pl.multiple_of(i * CHUNK, CHUNK), CHUNK)
+        normed, inverse = row_stats(x[rows, :].astype(F32))
+        upper = grad[rows, :]
+        weighted = upper * gains[0:1, :]
+        first = jnp.sum(weighted, axis=1, keepdims=True) * (1.0 / D)
+        second = jnp.sum(weighted * normed, axis=1, keepdims=True) * (1.0 / D)
+        value = (mid[rows, :] + inverse * (weighted - first - normed * second)).astype(BF)
+        for r in range(4):
+            send[r, rows, :] = value[:, r * 192 : r * 192 + 192]
+        parts = (upper * normed, upper)
+        return tuple(s + jnp.sum(v, axis=0, keepdims=True) for s, v in zip(sums, parts))
+
+    sums = lax.fori_loop(0, SLOTS // CHUNK, norm_one, (zero,) * 2)
+    for r, value in zip((0, 2), sums):
+        small[r : r + 1, :] = value
+    exchange_start(at, sends, send, land_in, in_s, in_r)
+    keep_in = pltpu.make_async_copy(send.at[at.z], land_in.at[at.z], in_s.at[3])
+    keep_in.start()
+    reduce.corner_sum(WQ)
+    reduce.along_sum(WO)
+    reduce.cross_sum(WQ)
+    reduce.along_sum(WQ)
+
+    for c in range(4):
+        small[6 + c : 7 + c, :] = sums_of[c]
+        small[10 + c : 11 + c, 0:QW] = sums_of[4 + c, :, 0:QW]
+    line[at.z] = small[...]
+    for k in (1, 2, 3):
+        to = lax.rem(at.z + k, 4)
+        sends.start(small, line.at[at.z], line_s.at[k - 1], line_r.at[at.z], at.zth(to))
+    for k in (1, 2, 3):
+        s = lax.rem(at.z + k, 4)
+        arrived(line.at[s], line_r.at[s], at.yn)
+    me = at.y * 4 + at.c
+    plane[me] = line[0] + line[1] + line[2] + line[3]
+    for k in range(1, 8):
+        to = lax.rem(me + k, 8)
+        sends.start(
+            plane.at[me], plane.at[me], plane_s.at[k - 1], plane_r.at[me], (lax.div(to, 4), at.z, lax.rem(to, 4))
+        )
+    for k in range(1, 8):
+        s = lax.rem(me + k, 8)
+        arrived(plane.at[s], plane_r.at[s], at.yn)
+    value = plane[0]
+    for s in range(1, 8):
+        value = value + plane[s]
+    total[...] = value
+    exchange_wait(at, land_out, ex_r)
+    exchange_wait(at, land_in, in_r)
+    keep_out.wait()
+    keep_in.wait()
+    sends.drain()
+
+
+def at_enter(at):
+    barrier = pltpu.get_barrier_semaphore()
+    me = at.y * 4 + at.c
+    peers = [at.zth(lax.rem(at.z + k, 4)) for k in (1, 2, 3)]
+    for k in range(1, 8):
+        to = lax.rem(me + k, 8)
+        peers.append((lax.div(to, 4), at.z, lax.rem(to, 4)))
+    for peer in peers:
+        pl.semaphore_signal(barrier, inc=1, device_id=peer, device_id_type=MESH)
+    pl.semaphore_wait(barrier, len(peers))
+
+
+SHARDS = ((96, QW), (96, 192), (96, 768), (192, 384))
+
+
+def run_backward(*operands):
+    sem = pltpu.SemaphoreType.DMA
+    vmem = pltpu.VMEM
+    shape = jax.ShapeDtypeStruct
+    stages = [(4, 2, 4), (2, 2, 4), (2, 2), (2, 4), (4,)]
+    return pl.pallas_call(
+        backward_kernel,
+        out_shape=[shape(s, F32) for s in SHARDS] + [shape((16, D), F32)] + [shape((4, SLOTS, 192), BF)] * 2,
+        in_specs=[pl.BlockSpec(memory_space=pl.ANY)] * (len(operands) - 1) + [pl.BlockSpec(memory_space=vmem)],
+        out_specs=[pl.BlockSpec(memory_space=vmem)] * 5 + [pl.BlockSpec(memory_space=pl.ANY)] * 2,
+        scratch_shapes=[vmem((3, 768, 768), BF), vmem((4, 1024, 192), BF)]
+        + [vmem(lead + s, BF) for lead in stages for s in SHARDS]
+        + [
+            vmem((4, SLOTS, 768), BF), vmem((4, SLOTS, 768), BF), vmem((SLOTS, D), BF), vmem((D, SLOTS), BF),
+            vmem((784, SLOTS), BF), vmem((784, SLOTS), BF), vmem((1024, SLOTS), BF), vmem((SLOTS, D), F32),
+            vmem((SLOTS, D), BF), vmem((2, 3, 2, BIG_SLOTS, BIG_SLOTS), BF), vmem((2, 3, 3, 128, 128), BF),
+            vmem((SLOTS, 1024), BF), vmem((SLOTS, D), F32), vmem((4, SLOTS, 192), BF), vmem((4, SLOTS, 192), BF),
+            vmem((16, D), F32), vmem((8, 1, D), F32), vmem((4, 16, D), F32), vmem((8, 16, D), F32),
+            sem((4, 12)), sem((4, 12)), sem((12,)), sem((12,)), sem((2, 2)), sem((4,)), sem((4,)), sem((4,)), sem((4,)),
+            sem((3,)), sem((4,)), sem((7,)), sem((8,)),
+        ],
+        compiler_params=pltpu.CompilerParams(collective_id=1, has_side_effects=True, vmem_limit_bytes=VMEM_LIMIT),
+    )(*operands)
+
+
+def prepare(layer_in, grad_out, crop_ids, w_qkv, w_out, w_fc1, w_fc2, norm_gains, all_biases):
+    pairs = layer_in.shape[0]
+    labels = lax.ppermute(crop_ids, ("row", "col"), [(r * 4 + c, c * 4 + r) for r in range(4) for c in range(4)])
+    sources = slot_sources(labels).reshape(-1, 1)
+    place = jnp.where(sources < 0, -1, (sources % 2) * TOK + sources // 2)
+
+    def packed(q, k, v):
+        zero = jnp.zeros(q.shape[:-1] + (HALF,), q.dtype)
+        return jnp.concatenate(
+            [q[..., :128], k[..., :128], v[..., :128], q[..., 128:], k[..., 128:], v[..., 128:], zero], axis=-1
+        )
+
+    wq = packed(w_qkv[:, 0], w_qkv[:, 1], w_qkv[:, 2])
+    bias = all_biases.reshape(10, D)
+    bq, bv = bias[2].reshape(4, 1, 192), bias[3].reshape(4, 1, 192)
+    qkv_bias = packed(bq, jnp.zeros_like(bq), bv)
+    return (
+        layer_in.reshape(pairs, 384), grad_out.reshape(pairs, 384), place,
+        wq, w_out, w_fc1, w_fc2, norm_gains.reshape(2, D), bias, qkv_bias,
+    )
+
+
+def local_fast(
+    layer_in, grad_out, crop_ids, w_qkv, w_out, w_fc1, w_fc2, norm_gains, all_biases,
+    first_qkv, second_qkv, first_out, second_out, first_fc1, second_fc1, first_fc2, second_fc2,
+    first_gains, second_gains, first_biases, second_biases,
+):
+    pairs = layer_in.shape[0]
+    operands = prepare(layer_in, grad_out, crop_ids, w_qkv, w_out, w_fc1, w_fc2, norm_gains, all_biases)
+    place = operands[2].reshape(1, -1)
+    kept = run_forward(*operands)
+    own_q, owned_out, owned_fc1, own_2, total, land_out, land_in = run_backward(*kept, operands[7])
+
+    back = (jnp.arange(2 * TOK, dtype=jnp.int32)[:, None] == place).astype(BF)
+
+    def to_tokens(value):
+        halves = dot(back, value.reshape(4 * SLOTS, 192))
+        return jnp.concatenate([halves[:pairs], halves[TOK : TOK + pairs]], axis=1).reshape(pairs, 1, 384)
+
+    def unpacked(value):
+        q = jnp.concatenate([value[:, 0:128], value[:, 384:448]], axis=1)
+        k = jnp.concatenate([value[:, 128:256], value[:, 448:512]], axis=1)
+        v = jnp.concatenate([value[:, 256:384], value[:, 512:576]], axis=1)
+        return q, k, v
+
+    owned_qkv = jnp.stack(unpacked(own_q), axis=1)
+    owned_fc2 = own_2.T
+    q_sums, _, v_sums = unpacked(total[10:14])
+    grad_gains = total[0:2].reshape(-1)
+    grad_biases = jnp.concatenate([
+        total[2:4].reshape(-1), q_sums.reshape(-1), v_sums.reshape(-1), total[4:10].reshape(-1)
+    ])
+    weight_squares = jnp.sum(total[14])
+    grad_norm = jnp.sqrt(weight_squares + jnp.sum(grad_gains * grad_gains) + jnp.sum(grad_biases * grad_biases))
+    factor = jnp.minimum(1.0, CLIP_NORM / grad_norm)
+    upd_qkv = adam_step(w_qkv, owned_qkv, first_qkv, second_qkv, D ** (-0.5), factor)
+    upd_out = adam_step(w_out, owned_out, first_out, second_out, (D // 24) ** (-0.5), factor)
+    upd_fc1 = adam_step(w_fc1, owned_fc1, first_fc1, second_fc1, D ** (-0.5), factor)
+    upd_fc2 = adam_step(w_fc2, owned_fc2, first_fc2, second_fc2, FF ** (-0.5), factor)
+    upd_gains = adam_step(norm_gains, grad_gains, first_gains, second_gains, 0.3, factor)
+    upd_biases = adam_step(all_biases, grad_biases, first_biases, second_biases, 0.3, factor)
+    return (
+        to_tokens(land_out), to_tokens(land_in), grad_norm,
+        *upd_qkv, *upd_out, *upd_fc1, *upd_fc2, *upd_gains, *upd_biases,
+    )
 
 
 def dot(a, b):
@@ -199,7 +1178,7 @@
     return value.astype(F32)
 
 
-def local(
+def local_plain(
     layer_in, grad_out, crop_ids, w_qkv, w_out, w_fc1, w_fc2, norm_gains, all_biases,
     first_qkv, second_qkv, first_out, second_out, first_fc1, second_fc1, first_fc2, second_fc2,
     first_gains, second_gains, first_biases, second_biases,
@@ -267,7 +1246,7 @@
     fc1 = P(("row", "dp"), "col")
     whole = P()
     return jax.shard_map(
-        local,
+        local_fast if mesh.shape["dp"] == 2 else local_plain,
         mesh=mesh,
         in_specs=(
             tokens, tokens, P(("dp", "row")), qkv, out, fc1, out, whole, whole,

time: 809 us -> 322 us (0.40)
  waiting for transfers between devices: 341 us -> 0.01 us
  Pallas kernels: 0 us -> 249 us
  matrix products: 141 us -> 8.93 us
  blocking collectives: 114 us -> 0 us
  other arithmetic: 84.7 us -> 32.1 us
  local copies, waits for them, and re-layouts: 74 us -> 21.5 us
  starting transfers between devices: 24.3 us -> 1.5 us
  between operations: 21.6 us -> 4.95 us
    pallas_call x0 -> x2, Pallas kernels: none -> 249 us  [the longest x1 131 us: run_backward(): pl.pallas_call(backward_kernel, out_shape=[shape(s, F32) for s in SHARDS]...]
    reduce_scatter x7 -> x0, waiting for transfers between devices: 193 us -> none  [scatter(): value = lax.psum_scatter(value, name, scatter_dimension=dim, tiled=True)]
    dot_general x16 -> x0, matrix products: 108 us -> none  [the longest x4 36.2 us: dot_nt(): lax.dot_general(a, b, (((1,), (1,)), ((), ())), preferred_element_type=F32)]
    all_gather x6 -> x0, blocking collectives: 74 us -> none  [gather(): value = lax.all_gather(value, name, axis=dim, tiled=True)]
    all_to_all x4 -> x0, waiting for transfers between devices: 58.9 us -> none  [the longest x2 50.4 us: to_slots(): got = lax.all_to_all(sent, 'row', 0, 0, tiled=True)]
    unnamed x23 -> x0, waiting for transfers between devices: 55.5 us -> none
    psum x1 -> x0, blocking collectives: 40.1 us -> none  [local(): lax.psum((g_gains, g_biases, local_squares), ('dp', 'row', 'col'))]
    all_gather x6 -> x0, waiting for transfers between devices: 33.9 us -> none  [gather(): value = lax.all_gather(value, name, axis=dim, tiled=True)]
  transfers between devices with their start and end apart: 23 -> 1, of which waited for: 15 -> 0; matrix products, arithmetic and copies ran while one was open for 25% -> 2% of each run, Pallas kernels for 0% -> 0%
where the time goes in v2:
time: 322 us; the launch traced here: 318 us
  Pallas kernels  249 us (77%)
  other arithmetic  32.1 us (10%)
  local copies, waits for them, and re-layouts  21.5 us (7%)
  matrix products  8.93 us (3%)
  between operations  4.95 us (2%)
    pallas_call x1, Pallas kernels, run_backward(): pl.pallas_call(backward_kernel, out_shape=[shape(s, F32) for s in SHARDS]...  131 us
    pallas_call x1, Pallas kernels, run_forward(): pl.pallas_call(forward_kernel, out_shape=[jax.ShapeDtypeStruct(s, t) for...  119 us
    add x18, other arithmetic, slot_sources(): out.append(start + jnp.arange(length, dtype=jnp.int32))  19.3 us
    dot_general x2, matrix products, dot(): return jnp.dot(a, b, preferred_element_type=F32)  8.93 us
    unnamed x50, local copies, waits for them, and re-layouts  7.3 us
  transfers between devices with their start and end apart: 1, of which 0 were waited for; matrix products, arithmetic and copies ran while one was open for 2% of the time, Pallas kernels for 0%

profile of v2, /device:TPU:0, one launch (start us, length us, event | category | flops | bytes accessed | tf_op | source)
XLA Modules:
  0.0 318.1 jit_solution(17954814225670622399)
XLA Ops:
  0.7 1.5 collective-permute-start
  2.2 1.0 slice_bitcast_fusion
  3.2 0.8 fusion.46
  4.2 1.4 reshape.397.biases
  5.6 0.6 reshape.396.gains
  6.2 0.9 copy.76.w2_in
  7.1 0.7 concatenate.47.qkv_bias
  7.8 0.8 concatenate.46.wq_in
  8.7 0.4 convert_reduce_fusion.1
  9.2 0.1 copy.71
  9.3 0.1 copy.69
  9.4 0.1 multiply_reduce_fusion.1
  9.5 0.1 copy.70
  9.6 0.1 multiply_reduce_fusion.3
  9.9 0.7 fusion.47
  10.6 0.7 fusion.48
  11.2 0.6 iota_add_fusion.23
  11.9 0.1 fusion.26
  12.1 0.6 fusion.49
  12.7 0.6 iota_add_fusion.1
  13.4 1.3 iota_add_fusion.15
  14.7 1.3 iota_add_fusion.17
  16.0 1.3 iota_add_fusion.19
  17.3 1.3 iota_add_fusion.21
  18.6 0.1 concatenate.44
  18.7 0.7 iota_add_fusion.14
  19.4 0.7 iota_add_fusion
  20.0 1.3 iota_add_fusion.6
  21.3 1.3 iota_add_fusion.8
  22.6 1.3 iota_add_fusion.10
  23.9 1.3 iota_add_fusion.12
  25.4 0.7 iota_add_fusion.29
  26.0 1.2 iota_add_fusion.27
  27.3 1.3 iota_add_fusion.4
  28.7 0.6 iota_add_fusion.26
  29.2 1.2 iota_add_fusion.24
  30.5 1.3 iota_add_fusion.2
  31.9 0.9 reshape.406
  32.9 2.0 fusion.6.place
  34.9 118.7 %shard_map.412 = (bf16[4,768,640]{2,1,0:T(8,128)(2,1)}, bf16[4,1024,192]{2,1,0:T(8,128)(2,1)}, bf16[4,768,768]{2,1,0:T(8,128)(2,1)}, bf16[4,768,768]{2,1,0:T(8,1...) custom-call(bf16[1035,384]{1,0:T(8,128)(2,1)} %bitcast.57, ...), custom_call_target="tpu_custom_call" | custom-call | tf_op jit(solution)/shard_map/pallas_call | solution.py:547
  153.6 130.6 %shard_map.413 = (f32[96,640]{1,0:T(8,128)}, f32[96,192]{1,0:T(8,128)}, f32[96,768]{1,0:T(8,128)}, f32[192,384]{1,0:T(8,128)}, f32[16,768]{1,0:T(8,128)}, /*inde...) custom-call(bf16[4,768,640]{2,1,0:T(8,128)(2,1)} %get-tuple-element.51.wq_h, ...), custom_call_target="tpu_custom_call" | custom-call | tf_op jit(solution)/shard_map/pallas_call | solution.py:987
  284.2 0.7 fusion.43
  284.9 0.7 fusion.44
  285.5 1.4 fusion.45
  287.0 0.8 slice.272
  287.8 1.3 slice_reduce_fusion
  289.1 0.9 fusion.41
  290.0 1.0 fusion.42
  291.3 0.6 multiply_reduce_fusion
  293.9 0.7 slice_multiply_fusion
  294.7 5.1 %fusion = f32[2080,192]{0,1:T(8,128)S(1)} fusion(bf16[2176,192]{1,0:T(8,128)(2,1)} %bitcast.60, s32[2176]{0:T(1024)S(1)} %fusion.18), kind=kOutput, calls=%fused_computation.1 | convolution fusion | flops 1742540800 | bytes 2441728 | tf_op jit(solution)/shard_map/dot_general | solution.py:1075
  299.8 0.3 fusion.39
  300.1 0.1 maximum_bitcast_fusion.1
  300.2 3.3 %copy.78 = f32[1035,1,384]{2,1,0:T(1,128)} copy(f32[1035,1,384]{0,2,1:T(8,128)S(1)} %maximum_bitcast_fusion.1) | data formatting | bytes 3179520
  303.5 3.9 %fusion.1 = f32[2080,192]{0,1:T(8,128)S(1)} fusion(bf16[2176,192]{1,0:T(8,128)(2,1)S(1)} %bitcast.59, s32[2176]{0:T(1024)S(1)} %fusion.18), kind=kOutput, calls=%fused_computation.2 | convolution fusion | flops 1742540800 | bytes 2441728 | tf_op jit(solution)/shard_map/dot_general | solution.py:1075
  307.3 0.3 fusion.40
  307.6 0.1 maximum_bitcast_fusion
  307.8 3.0 copy.77
  310.8 0.7 fusion.27
  311.6 0.6 fusion.29
  312.3 1.1 fusion.31
  313.5 1.1 fusion.33
  314.6 0.8 fusion.35
  315.4 1.1 fusion.37
  (97 shorter events, 1.3 us)
Async XLA Ops:
  0.7 5.0 %copy-start.18 = (f32[1536]{0:T(1024)S(1)}, f32[1536]{0:T(1024)}, u32[]{:S(2)}) copy-start(f32[1536]{0:T(1024)} %param.28) | copy-start | bytes 18436
  0.7 5.5 %copy-start.1 = (f32[384,192]{0,1:T(8,128)S(1)}, f32[384,192]{0,1:T(8,128)}, u32[]{:S(2)}) copy-start(f32[384,192]{0,1:T(8,128)} %param.27) | copy-start | bytes 884740
  0.7 7.9 %collective-permute-start = (s32[2070]{0:T(1024)}, s32[2070]{0:T(1024)S(1)}, u32[]{:S(2)}, u32[]{:S(2)}) collective-permute-start(s32[2070]{0:T(1024)} %param.23), channel_id=1, source_target_pairs={{0,0},{1,4},{2,8},{3,12},{4,1},{5,5},{6,9},{7,13},{8,2},{9,6},{10,... | collective-permute-start | bytes 24848 | tf_op jit(solution)/shard_map/ppermute | solution.py:1009
  300.2 3.3 %copy-start.21 = (bf16[4,544,192]{2,1,0:T(8,128)(2,1)S(1)}, bf16[4,544,192]{2,1,0:T(8,128)(2,1)}, u32[]{:S(2)}) copy-start(bf16[4,544,192]{2,1,0:T(8,128)(2,1)} %get-tuple-element.68) | copy-start | bytes 2506756
  307.7 3.1 copy-start.12
  307.8 3.1 copy-start.16
  307.8 3.1 copy-start.17
  307.8 3.8 %copy-start.19 = (f32[1536]{0:T(1024)S(1)}, f32[1536]{0:T(1024)}, u32[]{:S(2)}) copy-start(f32[1536]{0:T(1024)} %param.39) | copy-start | bytes 18436
  307.8 3.8 %copy-start.20 = (f32[1536]{0:T(1024)S(1)}, f32[1536]{0:T(1024)}, u32[]{:S(2)}) copy-start(f32[1536]{0:T(1024)} %param.38) | copy-start | bytes 18436
  307.8 4.4 %copy-start.4 = (f32[384,192]{0,1:T(8,128)S(1)}, f32[384,192]{0,1:T(8,128)}, u32[]{:S(2)}) copy-start(f32[384,192]{0,1:T(8,128)} %param.37) | copy-start | bytes 884740
  307.8 4.4 %copy-start.5 = (f32[384,192]{0,1:T(8,128)S(1)}, f32[384,192]{0,1:T(8,128)}, u32[]{:S(2)}) copy-start(f32[384,192]{0,1:T(8,128)} %param.36) | copy-start | bytes 884740
  307.8 4.4 %copy-start.11 = (f32[192,384]{1,0:T(8,128)S(1)}, f32[192,384]{1,0:T(8,128)}, u32[]{:S(2)}) copy-start(f32[192,384]{1,0:T(8,128)} %get-tuple-element.74) | copy-start | bytes 884740
  311.5 1.9 copy-start.2
  311.5 1.9 copy-start.6
  311.5 1.9 copy-start.7
  311.6 1.9 copy-start.10
  313.4 1.2 copy-start.3
  313.4 1.2 copy-start.13
  313.4 1.2 copy-start.14
  313.4 1.2 copy-start.15
  313.4 1.9 copy-start
  313.4 1.9 copy-start.8
  313.5 1.9 copy-start.9
